TPU v7x, 512 devices: a whole 4x4x16 slice. The times are simulated.
512 devices in a mesh: dom: 64 (over x, z), feat: 8 (over y, core).
Axes of the slice: x: 4, y: 4, z: 16, core: 2. Of those that a mesh axis runs over, the one named last changes fastest.
Arguments:
- node_feats: float32 [512, 131072], P('feat', 'dom'), may hold values from -6 to 6
- weight: float32 [512, 512], replicated, may hold values from -0.25 to 0.25
- tiles: float32 [1024, 4, 128, 128], P('dom'), may hold values from -0.25 to 0.25
- block_cols: int32 [1024, 4], P('dom'), may hold values from 0 to 47, as said below
- block_count: int32 [1024], P('dom'), may hold values from 2 to 4, as said below
- hub_ids: int32 [1024], replicated, may hold values from 0 to 131071, as said below
- hub_adj: float32 [1024, 131072], P(None, 'dom'), may hold values from -0.0234375 to 0.0234375
- cotangent: float32 [512, 131072], P('feat', 'dom'), may hold values from -6 to 6
Outputs:
- activated: float32 [512, 131072], P('feat', 'dom')
- feat_grad: float32 [512, 131072], P('feat', 'dom')
- weight_grad: float32 [512, 512], P('dom', 'feat')
Inputs may be any that keep to these rules, and one draw needn't show every extreme that they name: `block_count`: every row block uses 2 to 4 slots, and some row block uses all 4. `block_cols`: in every row block, slot 0 names a block of the previous index of dom (below 16) and slot 1 a block of the next index of dom (32 or more); further slots name any of the three. `hub_ids`: hub ids are distinct. The vertices of one index of dom (2048 of them) contain at most 64 hubs, and in every draw some index of dom contains exactly 64.
All inputs are finite; a program needn't handle non-finite values.
Results may differ from a plain program's by a relative error of at most 0.000084.
Values sent between devices are 32-bit elements; how exact they have to be, the bound alone decides.
A program may use at most 128 MiB of HBM per device.

v0:
```python
import math

import jax
import jax.numpy as jnp
from jax import lax
from jax.sharding import PartitionSpec as P


def padded(cells, sides, width):
    for axis, dim in sides:
        count = lax.axis_size(axis)
        head = lax.slice_in_dim(cells, 0, width, axis=dim)
        tail = lax.slice_in_dim(cells, cells.shape[dim] - width, cells.shape[dim], axis=dim)
        cells = jnp.concatenate(
            [
                lax.ppermute(tail, axis, [(i, (i + 1) % count) for i in range(count)]),
                cells,
                lax.ppermute(head, axis, [((i + 1) % count, i) for i in range(count)]),
            ],
            axis=dim,
        )
    return cells


def from_behind(value, axis, steps):
    count = lax.axis_size(axis)
    pairs = [(source, (source + steps) % count) for source in range(count)]
    return lax.ppermute(value, axis, pairs)


def local(node_feats, weight, tiles, block_cols, block_count, hub_ids, hub_adj, cotangent):
    highest = lax.Precision.HIGHEST
    width = node_feats.shape[0]
    rows = node_feats.shape[1]
    nblk = rows // 128
    slots = block_cols.shape[1]
    full_width = weight.shape[0]
    dom_count = lax.axis_size("dom")
    dom_index = lax.axis_index("dom")
    feat_index = lax.axis_index("feat")
    feats_all = lax.all_gather(node_feats, "feat", axis=0, tiled=True)
    w_cols = lax.dynamic_slice_in_dim(weight, feat_index * width, width, 1)
    proj = lax.dot_general(w_cols, feats_all, (((0,), (0,)), ((), ())), precision=highest)
    extended = padded(proj, (("dom", 1),), rows)
    ext_blocks = extended.reshape(width, 3 * nblk, 128)
    live = (jnp.arange(slots, dtype=jnp.int32)[None, :] < block_count[:, None]).astype(jnp.float32)
    picked = jnp.take(ext_blocks, block_cols, axis=1) * live[None, :, :, None]
    agg_blocks = jnp.einsum("fbkc,bkrc->fbr", picked, tiles, precision=highest).reshape(width, rows)
    owner = hub_ids // rows
    mine = owner == dom_index
    local_col = jnp.clip(hub_ids - owner * rows, 0, rows - 1)
    row_iota = jnp.arange(rows, dtype=jnp.int32)
    hub_own = jnp.take(proj, local_col, axis=1) * mine.astype(jnp.float32)[None, :]
    hub_vals = lax.psum(hub_own, "dom")
    agg = agg_blocks + jnp.dot(
        hub_vals, hub_adj, precision=highest, preferred_element_type=jnp.float32
    )
    sig = jax.nn.sigmoid(agg)
    activated = agg * sig
    grad_agg = cotangent * sig * (1.0 + agg * (1.0 - sig))
    contrib = jnp.einsum(
        "fbr,bkrc->fbkc", grad_agg.reshape(width, nblk, 128), tiles, precision=highest
    )
    contrib = (contrib * live[None, :, :, None]).reshape(width, nblk * slots, 128)
    target = (
        block_cols.reshape(-1)[:, None] == jnp.arange(3 * nblk, dtype=jnp.int32)[None, :]
    ).astype(jnp.float32)
    back_ext = jnp.einsum("fjc,jm->fmc", contrib, target, precision=highest).reshape(
        width, 3 * rows
    )
    from_right = from_behind(back_ext[:, :rows], "dom", -1)
    from_left = from_behind(back_ext[:, 2 * rows :], "dom", 1)
    grad_proj = back_ext[:, rows : 2 * rows] + from_right + from_left
    hub_part = lax.dot_general(grad_agg, hub_adj, (((1,), (1,)), ((), ())), precision=highest)
    hub_total = lax.psum(hub_part, "dom")
    placing = ((local_col[:, None] == row_iota[None, :]) & mine[:, None]).astype(jnp.float32)
    grad_proj = grad_proj + jnp.dot(
        hub_total, placing, precision=highest, preferred_element_type=jnp.float32
    )
    feat_grad = lax.psum_scatter(
        jnp.dot(w_cols, grad_proj, precision=highest, preferred_element_type=jnp.float32),
        "feat",
        scatter_dimension=0,
        tiled=True,
    )
    scale_total = 1.0 / math.sqrt(rows * dom_count)
    weight_terms = (
        lax.dot_general(feats_all, grad_proj, (((1,), (1,)), ((), ())), precision=highest)
        * scale_total
    )
    weight_full = lax.psum(weight_terms, "dom")
    rows_dom = full_width // dom_count
    weight_grad = lax.dynamic_slice_in_dim(weight_full, dom_index * rows_dom, rows_dom, 0)
    return (activated, feat_grad, weight_grad)


def solution(mesh):
    return jax.shard_map(
        local,
        mesh=mesh,
        in_specs=(
            P("feat", "dom"),
            P(),
            P("dom", None, None, None),
            P("dom", None),
            P("dom"),
            P(),
            P(None, "dom"),
            P("feat", "dom"),
        ),
        out_specs=(P("feat", "dom"), P("feat", "dom"), P("dom", "feat")),
        check_vma=False,
    )
```

profile of v0, /device:TPU:1, one launch (start us, length us, event | category | flops | bytes accessed | tf_op | source)
XLA Modules:
  0.0 937.8 jit_solution(10521717197724789878)
XLA Ops:
  7.2 0.0 all-gather.2.cloned.1.call-start
  7.2 0.7 all-gather.2.cloned.1.call-update
  7.9 0.0 all-reduce.4.cloned.1.call-start
  8.0 0.7 compare_select_fusion.1
  8.7 0.1 copy.20
  8.7 0.1 reshape.64
  8.8 0.7 compare_and_fusion.1
  9.5 0.7 fusion.39
  10.3 45.5 %all-gather.2.cloned.1.call-done = f32[512,2048]{1,0:T(8,128)} async-done(((f32[64,2048]{1,0:T(8,128)}), f32[512,2048]{1,0:T(8,128)}) %all-gather.2.cloned.1.call-update) | async-done | bytes 4194320 | tf_op jit(solution)/shard_map/all_gather | solution.py:41
  55.7 4.9 fusion.24
  60.6 7.8 collective-permute-start.1
  68.4 1.9 collective-permute-start
  70.4 0.1 copy.24
  70.4 0.1 copy.19
  70.5 0.1 eq.36
  70.6 0.1 fusion.29
  70.7 0.3 copy.23
  71.0 2.8 gather_fusion.1
  73.9 1.1 multiply_bitcast_fusion
  75.0 0.0 all-reduce.4.cloned.1.call-update
  75.0 0.2 all-reduce.6.cloned.1.call-start
  75.3 4.2 collective-permute-done.1
  79.4 7.2 collective-permute-done
  86.7 1.4 copy_bitcast_fusion.1
  88.1 2.0 gather_fusion
  90.1 7.5 fusion.11
  97.6 229.3 %all-reduce.4.cloned.1.call-done = f32[64,1024]{0,1:T(8,128)} async-done(((f32[64,1024]{0,1:T(8,128)}), f32[64,1024]{0,1:T(8,128)}) %all-reduce.4.cloned.1.call-update) | async-done | bytes 262160 | tf_op jit(solution)/shard_map/psum | solution.py:54
  326.9 7.8 convolution_add_fusion
  334.7 1.0 fusion.38
  335.8 0.1 copy.34
  335.9 2.5 convolution_multiply_fusion
  338.4 2.3 fusion.7
  340.7 0.5 copy.43
  341.2 1.0 fusion.41
  342.2 3.4 collective-permute-start.2
  345.6 2.1 collective-permute-start.3
  347.8 8.8 fusion.37
  356.6 0.0 all-reduce.6.cloned.1.call-update
  356.6 0.0 all-reduce.8.cloned.1.call-start
  356.7 258.5 %all-reduce.6.cloned.1.call-done = f32[64,1024]{1,0:T(8,128)} async-done(((f32[64,1024]{1,0:T(8,128)}), f32[64,1024]{1,0:T(8,128)}) %all-reduce.6.cloned.1.call-update) | async-done | bytes 262160 | tf_op jit(solution)/shard_map/psum | solution.py:75
  615.2 5.0 fusion.19
  620.2 4.8 fusion.14
  625.1 0.0 reduce-scatter.2.cloned.1.call-start
  625.1 5.1 fusion.22
  630.3 249.6 %all-reduce.8.cloned.1.call-done = f32[512,64]{0,1:T(8,128)} async-done(((f32[512,64]{0,1:T(8,128)}), f32[512,64]{0,1:T(8,128)}) %all-reduce.8.cloned.1.call-update) | async-done | bytes 131088 | tf_op jit(solution)/shard_map/psum | solution.py:91
  879.9 0.8 constant_dynamic-slice_fusion
  880.7 0.7 copy.27
  881.4 49.9 %reduce-scatter.2.cloned.1.call-done = f32[64,2048]{1,0:T(8,128)} async-done(((f32[512,2048]{1,0:T(8,128)}), f32[64,2048]{1,0:T(8,128)}) %reduce-scatter.2.cloned.1.call-update) | async-done | bytes 524304 | tf_op jit(solution)/shard_map/reduce_scatter | solution.py:80
  (23 shorter events, 0.1 us)
Async XLA Ops:
  7.2 48.6 %copy-start = (f32[512,512]{1,0:T(8,128)S(1)}, f32[512,512]{1,0:T(8,128)}, u32[]{:S(2)}) copy-start(f32[512,512]{1,0:T(8,128)} %param.9) | copy-start | bytes 3145732
  7.2 48.6 %all-gather.2.cloned.1.call-start = ((), (), s32[]{:S(2)}) async-start(), calls=%async_computation.1 | async-start | bytes 4718592 | tf_op jit(solution)/shard_map/all_gather | solution.py:41
  7.9 319.0 %all-reduce.4.cloned.1.call-start = ((), (), s32[]{:S(2)}) async-start(), calls=%async_computation.2 | async-start | bytes 1048576 | tf_op jit(solution)/shard_map/psum | solution.py:54
  10.2 60.1 %copy-start.4 = (s32[16,4]{0,1:T(4,128)S(1)}, s32[16,4]{0,1:T(4,128)}, u32[]{:S(2)}) copy-start(s32[16,4]{0,1:T(4,128)} %param.11) | copy-start | bytes 772
  10.3 60.4 %copy-start.5 = (s32[16]{0:T(128)S(1)}, s32[16]{0:T(128)}, u32[]{:S(2)}) copy-start(s32[16]{0:T(128)} %param.12) | copy-start | bytes 196
  60.6 18.8 %collective-permute-start.1 = (f32[64,2048]{1,0:T(8,128)S(1)}, f32[64,2048]{1,0:T(8,128)}, u32[]{:S(2)}, u32[]{:S(2)}) collective-permute-start(f32[64,2048]{1,0:T(8,128)S(1)} %fusion.24), channel_id=1, source_target_pairs={{8,0},{16,8},{24,16},{32,24},{40,32},{48,40},{56,48},{64,56},{72,6... | collective-permute-start | bytes 1572872 | tf_op jit(solution)/shard_map/ppermute | solution.py:18
  68.4 18.3 %collective-permute-start = (f32[64,2048]{1,0:T(8,128)S(1)}, f32[64,2048]{1,0:T(8,128)}, u32[]{:S(2)}, u32[]{:S(2)}) collective-permute-start(f32[64,2048]{1,0:T(8,128)S(1)} %fusion.24), channel_id=1, source_target_pairs={{0,8},{8,16},{16,24},{24,32},{32,40},{40,48},{48,56},{56,64},{64,7... | collective-permute-start | bytes 1572872 | tf_op jit(solution)/shard_map/ppermute | solution.py:16
  75.0 540.2 %all-reduce.6.cloned.1.call-start = ((), (), s32[]{:S(2)}) async-start(), calls=%async_computation.3 | async-start | bytes 524288 | tf_op jit(solution)/shard_map/psum | solution.py:75
  97.6 237.1 %copy-start.3 = (f32[64,2048]{1,0:T(8,128)S(1)}, f32[64,2048]{1,0:T(8,128)}, u32[]{:S(2)}) copy-start(f32[64,2048]{1,0:T(8,128)} %param.15) | copy-start | bytes 1572868
  326.9 8.9 copy-start.2
  335.9 11.9 %slice-start = ((s8[8388608]{0:T(1024)(128)(4,1)}), s8[4194304]{0:T(1024)(128)(4,1)S(1)}, s32[]{:S(2)}) async-start(s8[8388608]{0:T(1024)(128)(4,1)} %bitcast.49), calls=%async_computation.6 | async-start | bytes 8388608
  338.4 9.4 %slice-start.1 = ((s8[8388608]{0:T(1024)(128)(4,1)}), s8[4194304]{0:T(1024)(128)(4,1)S(1)}, s32[]{:S(2)}) async-start(s8[8388608]{0:T(1024)(128)(4,1)} %bitcast.49), calls=%async_computation.7 | async-start | bytes 8388608
  342.2 272.9 %collective-permute-start.2 = (f32[64,2048]{1,0:T(8,128)}, f32[64,2048]{1,0:T(8,128)}, u32[]{:S(2)}, u32[]{:S(2)}) collective-permute-start(f32[64,2048]{1,0:T(8,128)} %get-tuple-element.13), channel_id=1, source_target_pairs={{0,504},{8,0},{16,8},{24,16},{32,24},{40,32},{48,40},{56,48},{64,5... | collective-permute-start | bytes 1572872 | tf_op jit(solution)/shard_map/ppermute | solution.py:28
  345.6 269.6 %collective-permute-start.3 = (f32[64,2048]{1,0:T(8,128)}, f32[64,2048]{1,0:T(8,128)}, u32[]{:S(2)}, u32[]{:S(2)}) collective-permute-start(f32[64,2048]{1,0:T(8,128)} %get-tuple-element.14), channel_id=1, source_target_pairs={{0,8},{8,16},{16,24},{24,32},{32,40},{40,48},{48,56},{56,64},{64,7... | collective-permute-start | bytes 1572872 | tf_op jit(solution)/shard_map/ppermute | solution.py:28
  356.6 523.3 %all-reduce.8.cloned.1.call-start = ((), (), s32[]{:S(2)}) async-start(), calls=%async_computation.5 | async-start | bytes 262144 | tf_op jit(solution)/shard_map/psum | solution.py:91
  615.2 5.0 copy-start.1
  625.1 306.3 %reduce-scatter.2.cloned.1.call-start = ((), (), s32[]{:S(2)}) async-start(), calls=%async_computation.4 | async-start | bytes 4718592 | tf_op jit(solution)/shard_map/reduce_scatter | solution.py:80
Sparse Core Ops, SparseCore 0:
  10.2 45.5 all-gather.1
  75.1 251.7 all-reduce.3
  356.7 258.3 all-reduce.5
  625.2 254.6 all-reduce.7
  883.2 48.0 reduce-scatter.1
where the time goes:
time: 940 us; the launch traced here: 938 us
  waiting for transfers between devices  845 us (90%)
  matrix products  48.7 us (5%)
  starting transfers between devices  15.6 us (2%)
  between operations  14 us (1%)
    psum x1, waiting for transfers between devices, local(): hub_total = lax.psum(hub_part, 'dom')  259 us
    psum x1, waiting for transfers between devices, local(): weight_full = lax.psum(weight_terms, 'dom')  250 us
    psum x1, waiting for transfers between devices, local(): hub_vals = lax.psum(hub_own, 'dom')  229 us
    reduce_scatter x1, waiting for transfers between devices, local(): lax.psum_scatter(jnp.dot(w_cols, grad_proj, precision=highest, preferred_...  49.9 us
    all_gather x1, waiting for transfers between devices, local(): feats_all = lax.all_gather(node_feats, 'feat', axis=0, tiled=True)  45.5 us
  transfers between devices with their start and end apart: 9, of which 7 were waited for; matrix products, arithmetic and copies ran while one was open for 4% of the time, Pallas kernels for 0%

commit v1 on v0

v1 whole, which is shorter than its diff:
```python
import functools
import math

import jax
import jax.numpy as jnp
from jax import lax
from jax.experimental import pallas as pl
from jax.experimental.pallas import tpu as pltpu
from jax.sharding import PartitionSpec as P

MESH = pl.DeviceIdType.MESH
F32 = jnp.float32
BF16 = jnp.bfloat16
NN = (((1,), (0,)), ((), ()))
NT = (((1,), (1,)), ((), ()))


def split(value):
    high = value.astype(BF16)
    low = (value - high.astype(F32)).astype(BF16)
    return high, low


def mm(a, b, dims):
    return lax.dot_general(a, b, dims, preferred_element_type=F32)


def stacked(value):
    high, low = split(value)
    return jnp.concatenate([high, low], axis=0)


def mm3(left, right_high, right_low, dims):
    rows = left.shape[0] // 2
    both = mm(left, right_high, dims)
    return both[:rows] + both[rows:] + mm(left[:rows], right_low, dims)


def kernel(
    sizes,
    x, w, tiles, hub_adj, cot, ids, cols, live, ent, keep, last, has,
    act, fg, wg,
    ext, adj_f32, adj_hi, adj_lo, tiles_f32, cat_hi, cat_lo, pick,
    w_f32, w_st, wt_st, y_send, y_all, cot_all, act_send, q_send, q_all,
    hub_acc, hub_in, contrib, runs, b_send, b_recv, fg_out,
    h_src, h_rx, h_zsrc, h_rz, h_zg, h_xg,
    wg_src, wg_recv, wg_xsrc, wg_rx, wg_zsrc, wg_rz,
    s_x, s_misc, s_adj, s_cot_own, s_out,
    s_nbr, s_cot, s_y, s_q, s_act, s_back, s_hx, s_hz, s_hzg, s_hxg, s_wf, s_wx, s_wz,
):
    nx, nz, nf, nb, slots = sizes
    nd = nx * nz
    fl, vl = x.shape
    full = w.shape[0]
    nh = hub_adj.shape[0]
    pb = nb // nf
    vw = pb * 128
    row_tiles = fl // 8
    per_q = nh // 128 // nx
    dom = lax.axis_index("dom")
    me = lax.axis_index("feat")
    my_x, my_z = dom // nz, dom % nz
    nxt, prv = (dom + 1) % nd, (dom + nd - 1) % nd

    def feat_peer(k):
        return (me + k) % nf

    def feat_from(k):
        return (me + nf - k) % nf

    def x_peer(k):
        return (my_x + k) % nx

    def z_peer(k):
        return (my_z + k) % nz

    def z_from(k):
        return (my_z + nz - k) % nz

    def to(domain, feature):
        return {"dom": domain, "feat": feature}

    def x_dev(k):
        return to(x_peer(k) * nz + my_z, me)

    def z_dev(k):
        return to(my_x * nz + z_peer(k), me)

    def f_dev(k):
        return to(dom, feat_peer(k))

    def remote(src, dst, sems, at, device):
        return pltpu.make_async_remote_copy(
            src_ref=src, dst_ref=dst, send_sem=sems.at[0, at], recv_sem=sems.at[1, at],
            device_id=device, device_id_type=MESH,
        )

    def loop(lower, upper, body):
        def step(i, carry):
            body(i)
            return carry

        lax.fori_loop(lower, upper, step, 0)

    x_loads = [
        pltpu.make_async_copy(x.at[:, pl.ds(128 * b, 128)], ext.at[nb + b], s_x.at[b])
        for b in range(nb)
    ]
    for copy in x_loads:
        copy.start()
    tiles_load = pltpu.make_async_copy(tiles, tiles_f32, s_misc.at[0])
    w_load = pltpu.make_async_copy(w, w_f32, s_misc.at[1])
    adj_loads = [
        pltpu.make_async_copy(hub_adj.at[:, pl.ds(vw * p, vw)], adj_f32.at[p], s_adj.at[p])
        for p in range(nf)
    ]
    cot_own = pltpu.make_async_copy(
        cot.at[:, pl.ds(pl.multiple_of(vw * me, 128), vw)],
        cot_all.at[pl.ds(pl.multiple_of(fl * me, 8), fl), :], s_cot_own,
    )
    tiles_load.start()
    w_load.start()
    cot_own.start()
    for copy in adj_loads:
        copy.start()

    barrier = pltpu.get_barrier_semaphore()

    def greet(device):
        pl.semaphore_signal(barrier, inc=1, device_id=device, device_id_type=MESH)

    greet(to(nxt, me))
    greet(to(prv, me))
    for k in range(1, nx):
        greet(x_dev(k))
    loop(1, nz, lambda k: greet(z_dev(k)))
    loop(1, nf, lambda k: greet(f_dev(k)))
    pl.semaphore_wait(barrier, 2 + (nx - 1) + (nz - 1) + (nf - 1))

    for copy in x_loads:
        copy.wait()
    mine = ext.at[pl.ds(nb, nb)]
    to_nxt = remote(mine, ext.at[pl.ds(0, nb)], s_nbr, 0, to(nxt, me))
    to_prv = remote(mine, ext.at[pl.ds(2 * nb, nb)], s_nbr, 1, to(prv, me))
    to_nxt.start()
    to_prv.start()

    def cot_copy(k):
        p = feat_peer(k)
        return remote(
            cot.at[:, pl.ds(pl.multiple_of(vw * p, 128), vw)],
            cot_all.at[pl.ds(pl.multiple_of(fl * me, 8), fl), :], s_cot, k - 1, f_dev(k),
        )

    local_id = ids[...] - dom * vl
    hub_acc[...] = jnp.zeros_like(hub_acc)

    def own_hubs(p):
        row = lax.broadcasted_iota(jnp.int32, (vw, nh), 0) + p * vw
        chunk = jnp.where(row == local_id, 1.0, 0.0).astype(BF16)
        pick[p] = chunk
        left = stacked(jnp.concatenate([ext[nb + pb * p + j] for j in range(pb)], axis=1))
        both = mm(left, chunk, NN)
        hub_acc[...] += both[:fl] + both[fl:]

    loop(0, nf, own_hubs)

    def x_rs_copy(s, k):
        return remote(h_src.at[s, x_peer(k)], h_rx.at[s, k - 1], s_hx.at[s], k - 1, x_dev(k))

    def z_rs_copy(s, k):
        return remote(h_zsrc.at[s, z_peer(k)], h_rz.at[s, k - 1], s_hz.at[s], k - 1, z_dev(k))

    def z_ag_copy(s, k):
        return remote(h_zg.at[s, my_z], h_zg.at[s, my_z], s_hzg.at[s], k - 1, z_dev(k))

    def z_ag_recv(s, k):
        at = h_zg.at[s, z_from(k)]
        return remote(at, at, s_hzg.at[s], k - 1, z_dev(k))

    def x_ag_copy(s, k):
        return remote(h_zg.at[s], h_xg.at[s, my_x], s_hxg.at[s], k - 1, x_dev(k))

    def x_ag_recv(s, k):
        return remote(
            h_zg.at[s], h_xg.at[s, (my_x + nx - k) % nx], s_hxg.at[s], k - 1, x_dev(k)
        )

    def hub_start(s):
        for q in range(nx):
            for i in range(nz):
                r, c = i // per_q, q * per_q + i % per_q
                h_src[s, q, i] = hub_acc[8 * r : 8 * r + 8, 128 * c : 128 * c + 128]
        for k in range(1, nx):
            x_rs_copy(s, k).start()

    def hub_z(s):
        for k in range(1, nx):
            x_rs_copy(s, k).wait_recv()
        total = h_src[s, my_x]
        for k in range(1, nx):
            total += h_rx[s, k - 1]
        h_zsrc[s] = total
        loop(1, nz, lambda k: z_rs_copy(s, k).start())

    def hub_zg(s):
        loop(1, nz, lambda k: z_rs_copy(s, k).wait_recv())
        total = h_zsrc[s, my_z]
        for k in range(1, nz):
            total += h_rz[s, k - 1]
        h_zg[s, my_z] = total
        loop(1, nz, lambda k: z_ag_copy(s, k).start())

    def hub_xg(s):
        loop(1, nz, lambda k: z_ag_recv(s, k).wait_recv())
        for k in range(1, nx):
            x_ag_copy(s, k).start()
        h_xg[s, my_x] = h_zg[s]

    def hub_end(s):
        for k in range(1, nx):
            x_ag_recv(s, k).wait_recv()
        for q in range(nx):
            for i in range(nz):
                r, c = i // per_q, q * per_q + i % per_q
                high, low = split(h_xg[s, q, i])
                hub_acc[8 * r : 8 * r + 8, 128 * c : 128 * c + 128] = h_xg[s, q, i]
        hub_in[...] = stacked(hub_acc[...])

    hub_start(0)
    loop(1, nf, lambda k: cot_copy(k).start())

    tiles_load.wait()

    def split_tiles(b):
        both = [split(tiles_f32[b, k]) for k in range(slots)]
        cat_hi[b] = jnp.concatenate([one[0] for one in both], axis=1)
        cat_lo[b] = jnp.concatenate([one[1] for one in both], axis=1)

    loop(0, nb, split_tiles)
    hub_z(0)

    w_load.wait()
    w_st[...] = stacked(w_f32[...])
    wt_st[...] = stacked(w_f32[...].T)

    def split_adj(p):
        high, low = split(adj_f32[p])
        adj_hi[p] = high
        adj_lo[p] = low

    for copy in adj_loads:
        copy.wait()
    loop(0, nf // 2, split_adj)
    hub_zg(0)
    loop(nf // 2, nf, split_adj)
    hub_xg(0)

    to_nxt.wait_recv()
    to_prv.wait_recv()

    def tile_part(p):
        for j in range(pb):
            b = p * pb + j
            left = jnp.concatenate(
                [ext[cols[b * slots + k]] * live[b * slots + k] for k in range(slots)], axis=1
            )
            y_send[p, :, 128 * j : 128 * j + 128] = mm3(stacked(left), cat_hi[b], cat_lo[b], NT)

    loop(0, nf, tile_part)
    hub_end(0)

    def y_copy(k):
        return remote(
            y_send.at[feat_peer(k)], y_all.at[pl.ds(pl.multiple_of(fl * me, 8), fl), :],
            s_y, k - 1, f_dev(k),
        )

    def y_recv(k):
        at = y_all.at[pl.ds(pl.multiple_of(fl * feat_from(k), 8), fl), :]
        return remote(y_send.at[0], at, s_y, k - 1, f_dev(k))

    def hub_to_y(p):
        return y_send[p] + mm3(hub_in[...], adj_hi[p], adj_lo[p], NN)

    def hub_part(k):
        p = feat_peer(k)
        y_send[p] = hub_to_y(p)
        y_copy(k).start()

    loop(1, nf, hub_part)
    y_all[pl.ds(pl.multiple_of(fl * me, 8), fl), :] = hub_to_y(me)

    loop(1, nf, lambda k: y_recv(k).wait_recv())
    y_hi, y_lo = split(y_all[...])
    agg = mm3(wt_st[...], y_hi, y_lo, NN)
    sig = 1.0 / (1.0 + jnp.exp(-agg))
    act_send[...] = agg * sig
    cot_own.wait()

    def cot_recv(k):
        at = cot_all.at[pl.ds(pl.multiple_of(fl * feat_from(k), 8), fl), :]
        return remote(cot.at[:, pl.ds(0, vw)], at, s_cot, k - 1, f_dev(k))

    loop(1, nf, lambda k: cot_recv(k).wait_recv())
    grad = cot_all[...] * sig * (1.0 + agg * (1.0 - sig))
    g_hi, g_lo = split(grad)
    q_send[...] = mm3(w_st[...], g_hi, g_lo, NN)

    def rows_of(ref, p):
        return ref.at[pl.ds(pl.multiple_of(fl * p, 8), fl), :]

    def q_copy(k):
        return remote(rows_of(q_send, feat_peer(k)), q_all.at[me], s_q, k - 1, f_dev(k))

    def q_recv(k):
        return remote(rows_of(q_send, me), q_all.at[feat_from(k)], s_q, k - 1, f_dev(k))

    loop(1, nf, lambda k: q_copy(k).start())
    q_all[me] = q_send[pl.ds(pl.multiple_of(fl * me, 8), fl), :]

    g_st = jnp.concatenate([g_hi, g_lo], axis=0)
    terms = mm3(g_st, y_hi, y_lo, NT)
    for p in range(nf):
        wg_src[p] = terms[fl * p : fl * p + fl]

    def wf_copy(k):
        return remote(wg_src.at[feat_peer(k)], wg_recv.at[k - 1], s_wf, k - 1, f_dev(k))

    loop(1, nf, lambda k: wf_copy(k).start())

    def act_at(p):
        return act.at[:, pl.ds(pl.multiple_of(vw * p, 128), vw)]

    def act_copy(k):
        return remote(rows_of(act_send, feat_peer(k)), act_at(me), s_act, k - 1, f_dev(k))

    def act_recv(k):
        return remote(rows_of(act_send, me), act_at(feat_from(k)), s_act, k - 1, f_dev(k))

    loop(1, nf, lambda k: act_copy(k).start())
    act_own = pltpu.make_async_copy(rows_of(act_send, me), act_at(me), s_misc.at[2])
    act_own.start()

    def hub_back(p):
        left = stacked(q_all[p])
        return mm3(left, adj_hi[p], adj_lo[p], NT)

    hub_acc[...] = hub_back(me)

    def hub_step(k):
        q_recv(k).wait_recv()
        hub_acc[...] += hub_back(feat_from(k))

    loop(1, nf, hub_step)
    hub_start(1)

    def slot_terms(p):
        for j in range(pb):
            b = p * pb + j
            left = stacked(q_all[p, :, 128 * j : 128 * j + 128])
            out = mm3(left, cat_hi[b], cat_lo[b], NN)
            for k in range(slots):
                contrib[b * slots + k] = out[:, 128 * k : 128 * k + 128]

    loop(0, nf, slot_terms)

    def run_step(j, total):
        total = total * keep[j] + contrib[ent[j]]
        runs[j] = total
        return total

    lax.fori_loop(0, nb * slots, run_step, jnp.zeros((fl, 128), F32))

    def back_send(b):
        b_send[0, b] = runs[last[b]] * has[b]
        b_send[1, b] = runs[last[2 * nb + b]] * has[2 * nb + b]

    loop(0, nb, back_send)
    back_prv = remote(b_send.at[0], b_recv.at[0], s_back, 0, to(prv, me))
    back_nxt = remote(b_send.at[1], b_recv.at[1], s_back, 1, to(nxt, me))
    back_prv.start()
    back_nxt.start()

    hub_z(1)
    hub_zg(1)

    loop(1, nf, lambda k: wf_copy(k).wait_recv())
    term = wg_src[me]
    for k in range(1, nf):
        term += wg_recv[k - 1]
    part = full // nx
    for q in range(nx):
        wg_xsrc[q] = term[:, part * q : part * q + part]

    def wx_copy(k):
        return remote(wg_xsrc.at[x_peer(k)], wg_rx.at[k - 1], s_wx, k - 1, x_dev(k))

    for k in range(1, nx):
        wx_copy(k).start()

    hub_xg(1)

    for k in range(1, nx):
        wx_copy(k).wait_recv()
    term = wg_xsrc[my_x]
    for k in range(1, nx):
        term += wg_rx[k - 1]
    term = term.T
    lanes = wg_zsrc.shape[2]
    if lanes > fl:
        term = jnp.concatenate([term, jnp.zeros((part, lanes - fl), F32)], axis=1)
    wg_zsrc[...] = term.reshape(wg_zsrc.shape)

    def wz_copy(k):
        return remote(wg_zsrc.at[z_peer(k)], wg_rz.at[k - 1], s_wz, k - 1, z_dev(k))

    loop(1, nz, lambda k: wz_copy(k).start())

    hub_end(1)
    back_prv.wait_recv()
    back_nxt.wait_recv()

    def out_copy(p):
        return pltpu.make_async_copy(
            fg_out.at[p], fg.at[:, pl.ds(pl.multiple_of(vw * p, 128), vw)], s_out.at[p]
        )

    def finish(p):
        both = mm(hub_in[...], pick[p], NT)
        placed = both[:fl] + both[fl:]
        for j in range(pb):
            b = p * pb + j
            own = runs[last[nb + b]] * has[nb + b]
            total = placed[:, 128 * j : 128 * j + 128] + own + b_recv[0, b] + b_recv[1, b]
            fg_out[p, :, 128 * j : 128 * j + 128] = total
        out_copy(p).start()

    loop(0, nf, finish)

    loop(1, nz, lambda k: wz_copy(k).wait_recv())
    term = wg_zsrc[my_z]
    for k in range(1, nz):
        term += wg_rz[k - 1]
    wg[...] = term[:, :fl] * (1.0 / math.sqrt(vl * nd))

    act_own.wait()
    loop(1, nf, lambda k: act_recv(k).wait_recv())
    to_nxt.wait_send()
    to_prv.wait_send()
    back_prv.wait_send()
    back_nxt.wait_send()

    def feat_sent(k):
        cot_copy(k).wait_send()
        y_copy(k).wait_send()
        q_copy(k).wait_send()
        wf_copy(k).wait_send()
        act_copy(k).wait_send()

    loop(1, nf, feat_sent)
    for k in range(1, nx):
        for s in range(2):
            x_rs_copy(s, k).wait_send()
            x_ag_copy(s, k).wait_send()
        wx_copy(k).wait_send()

    def z_sent(k):
        for s in range(2):
            z_rs_copy(s, k).wait_send()
            z_ag_copy(s, k).wait_send()
        wz_copy(k).wait_send()

    loop(1, nz, z_sent)
    loop(0, nf, lambda p: out_copy(p).wait())


def local(nd, nf, nx, node_feats, weight, tiles, block_cols, block_count, hub_ids, hub_adj, cotangent):
    nz = nd // nx
    fl, vl = node_feats.shape
    full = weight.shape[0]
    nb, slots = block_cols.shape
    nh = hub_adj.shape[0]
    vw = vl // nf
    entries = nb * slots

    col = block_cols.reshape(-1)
    alive = (jnp.arange(slots, dtype=jnp.int32)[None, :] < block_count[:, None]).reshape(-1)
    target = jnp.where(alive, col, 3 * nb)
    at = jnp.arange(entries, dtype=jnp.int32)
    before = target[None, :] * entries + at[None, :] < target[:, None] * entries + at[:, None]
    rank = jnp.sum(before.astype(jnp.int32), axis=1)
    placed = rank[:, None] == at[None, :]
    ent = jnp.sum(jnp.where(placed, at[:, None], 0), axis=0)
    repeat = jnp.any((target[None, :] == target[:, None]) & (at[None, :] < at[:, None]), axis=1)
    keep = jnp.sum(jnp.where(placed & repeat[:, None], 1.0, 0.0), axis=0)
    blocks = jnp.arange(3 * nb, dtype=jnp.int32)
    upto = jnp.sum((target[:, None] <= blocks[None, :]).astype(jnp.int32), axis=0)
    last = jnp.maximum(upto - 1, 0)
    has = jnp.any(target[:, None] == blocks[None, :], axis=0).astype(F32)
    live = alive.astype(F32)

    lanes = max(fl, 128)
    vm = pltpu.VMEM
    dma = pltpu.SemaphoreType.DMA
    hub_tile = (8, 128)
    scratch = [
        vm((3 * nb, fl, 128), F32),
        vm((nf, nh, vw), F32), vm((nf, nh, vw), BF16), vm((nf, nh, vw), BF16),
        vm((nb, slots, 128, 128), F32),
        vm((nb, 128, slots * 128), BF16), vm((nb, 128, slots * 128), BF16),
        vm((nf, vw, nh), BF16),
        vm((full, full), F32), vm((2 * full, full), BF16), vm((2 * full, full), BF16),
        vm((nf, fl, vw), F32), vm((full, vw), F32), vm((full, vw), F32), vm((full, vw), F32),
        vm((full, vw), F32), vm((nf, fl, vw), F32),
        vm((fl, nh), F32), vm((2 * fl, nh), BF16),
        vm((entries, fl, 128), F32), vm((entries, fl, 128), F32),
        vm((2, nb, fl, 128), F32), vm((2, nb, fl, 128), F32), vm((nf, fl, vw), F32),
        vm((2, nx, nz) + hub_tile, F32), vm((2, nx - 1, nz) + hub_tile, F32),
        vm((2, nz) + hub_tile, F32), vm((2, nz - 1) + hub_tile, F32),
        vm((2, nz) + hub_tile, F32), vm((2, nx, nz) + hub_tile, F32),
        vm((nf, fl, full), F32), vm((nf - 1, fl, full), F32),
        vm((nx, fl, full // nx), F32), vm((nx - 1, fl, full // nx), F32),
        vm((nz, full // nx // nz, lanes), F32), vm((nz - 1, full // nx // nz, lanes), F32),
        dma((nb,)), dma((3,)), dma((nf,)), dma, dma((nf,)),
        dma((2, 2)), dma((2, nf - 1)), dma((2, nf - 1)), dma((2, nf - 1)), dma((2, nf - 1)),
        dma((2, 2)),
        dma((2, 2, nx - 1)), dma((2, 2, nz - 1)), dma((2, 2, nz - 1)), dma((2, 2, nx - 1)),
        dma((2, nf - 1)), dma((2, nx - 1)), dma((2, nz - 1)),
    ]
    hbm = pl.BlockSpec(memory_space=pl.ANY)
    vmem = pl.BlockSpec(memory_space=pltpu.VMEM)
    smem = pl.BlockSpec(memory_space=pltpu.SMEM)
    return pl.pallas_call(
        functools.partial(kernel, (nx, nz, nf, nb, slots)),
        out_shape=(
            jax.ShapeDtypeStruct((fl, vl), F32),
            jax.ShapeDtypeStruct((fl, vl), F32),
            jax.ShapeDtypeStruct((full // nd, fl), F32),
        ),
        in_specs=[hbm] * 5 + [vmem] + [smem] * 6,
        out_specs=(hbm, hbm, vmem),
        scratch_shapes=scratch,
        compiler_params=pltpu.CompilerParams(
            collective_id=0, has_side_effects=True, vmem_limit_bytes=60 * 1024 * 1024
        ),
    )(
        node_feats, weight, tiles, hub_adj, cotangent, hub_ids.reshape(1, nh),
        col, live, ent, keep, last, has,
    )


def solution(mesh):
    nd, nf = mesh.shape["dom"], mesh.shape["feat"]
    nx = 4 if nd == 64 else 2
    return jax.shard_map(
        functools.partial(local, nd, nf, nx),
        mesh=mesh,
        in_specs=(
            P("feat", "dom"),
            P(),
            P("dom", None, None, None),
            P("dom", None),
            P("dom"),
            P(),
            P(None, "dom"),
            P("feat", "dom"),
        ),
        out_specs=(P("feat", "dom"), P("feat", "dom"), P("dom", "feat")),
        check_vma=False,
    )
```

time: 940 us -> 125 us (0.13)
  waiting for transfers between devices: 845 us -> 0 us
  Pallas kernels: 0 us -> 114 us
  matrix products: 48.7 us -> 0 us
  starting transfers between devices: 15.6 us -> 0 us
  between operations: 14 us -> 0.67 us
    psum x3 -> x0, waiting for transfers between devices: 737 us -> none  [the longest x1 259 us: local(): hub_total = lax.psum(hub_part, 'dom')]
    pallas_call x0 -> x1, Pallas kernels: none -> 114 us  [local(): pl.pallas_call(functools.partial(kernel, (nx, nz, nf, nb, slots)), out_sh...]
    reduce_scatter x1 -> x0, waiting for transfers between devices: 49.9 us -> none  [local(): lax.psum_scatter(jnp.dot(w_cols, grad_proj, precision=highest, preferred_...]
    dot_general x9 -> x0, matrix products: 48.7 us -> none  [the longest x1 8.78 us: local(): lax.dot_general(grad_agg, hub_adj, (((1,), (1,)), ((), ())), precision=hi...]
    all_gather x1 -> x0, waiting for transfers between devices: 45.5 us -> none  [local(): feats_all = lax.all_gather(node_feats, 'feat', axis=0, tiled=True)]
    ppermute x4 -> x0, starting transfers between devices: 15.2 us -> none  [the longest x1 7.79 us: padded(): lax.ppermute(head, axis, [((i + 1) % count, i) for i in range(count)])]
    ppermute x4 -> x0, waiting for transfers between devices: 11.4 us -> none  [the longest x1 7.22 us: padded(): lax.ppermute(tail, axis, [(i, (i + 1) % count) for i in range(count)])]
  transfers between devices with their start and end apart: 9 -> 0, of which waited for: 7 -> 0; matrix products, arithmetic and copies ran while one was open for 4% -> 0% of each run, Pallas kernels for 0% -> 0%
where the time goes in v1:
time: 125 us
  Pallas kernels  114 us (91%)
  local copies, waits for them, and re-layouts  5.96 us (5%)
  other arithmetic  4.2 us (3%)
    pallas_call x1, Pallas kernels, local(): pl.pallas_call(functools.partial(kernel, (nx, nz, nf, nb, slots)), out_sh...  114 us
    unnamed x6, local copies, waits for them, and re-layouts  5.77 us

profile of v1, /device:TPU:1, one launch (start us, length us, event | category | flops | bytes accessed | tf_op | source)
XLA Modules:
  0.0 125.1 jit_solution(13958247706407597955)
XLA Ops:
  0.6 0.7 iota_compare_fusion.4
  1.4 0.1 lt.56
  1.5 0.5 convert_element_type.12.live
  2.0 0.8 copy.13
  2.7 0.1 reshape.80.cols
  2.8 0.0 copy-start
  2.9 0.2 convert_reduce_fusion
  3.0 0.6 select_reduce_fusion.1.ent
  3.6 0.1 convert_reduce_fusion.1
  3.8 0.6 add_maximum_fusion.last
  4.3 0.2 fusion.2
  4.5 0.6 select_reduce_fusion.keep
  5.1 0.1 fusion.3
  5.2 0.6 convert_element_type.15.has
  5.8 0.0 copy-done
  5.8 114.3 %shard_map.103 = (f32[64,2048]{1,0:T(8,128)}, f32[64,2048]{1,0:T(8,128)}, f32[8,64]{1,0:T(8,128)}) custom-call(f32[64,2048]{1,0:T(8,128)} %x.1, f32[512,512]{1,0:T(8,128)} %w.1, f32[16,4,128,128]{3,2,1,0:T(8,128)} %tiles.1, f32[1024,2048]{1,0:T(8,128)} %hub_adj.1, f32[64,2048]{1,0:T(8,128)} %cot.1, s32[1,1024]{1,0:T(1,128)} %bitcast.1, s32[64]{0:T(128)} %copy-done, ...), custom_call_target="tpu_custom_call" | custom-call | tf_op jit(solution)/shard_map/pallas_call | solution.py:534
  120.1 1.9 %copy.17 = f32[64,2048]{1,0:T(8,128)} copy(f32[64,2048]{1,0:T(8,128)} %get-tuple-element.8) | data formatting | bytes 1048576
  122.0 1.9 %copy.18 = f32[64,2048]{1,0:T(8,128)} copy(f32[64,2048]{1,0:T(8,128)} %get-tuple-element.9) | data formatting | bytes 1048576
  123.9 1.3 %copy.19 = f32[8,64]{1,0:T(8,128)} copy(f32[8,64]{1,0:T(8,128)} %get-tuple-element.10) | data formatting | bytes 4096
  (1 shorter events, 0.0 us)
Async XLA Ops:
  2.8 3.0 %copy-start = (s32[64]{0:T(128)}, s32[64]{0:T(128)S(1)}, u32[]{:S(2)}) copy-start(s32[64]{0:T(128)S(1)} %reshape.80.cols) | copy-start | bytes 772

commit v2 on v1

--- a/solution.py
+++ b/solution.py
@@ -37,18 +37,20 @@
 
 
 def kernel(
-    sizes,
-    x, w, tiles, hub_adj, cot, ids, cols, live, ent, keep, last, has,
+    sizes, groups,
+    x, w, tiles, hub_adj, cot, ids, cols_v, cols, count,
     act, fg, wg,
     ext, adj_f32, adj_hi, adj_lo, tiles_f32, cat_hi, cat_lo, pick,
     w_f32, w_st, wt_st, y_send, y_all, cot_all, act_send, q_send, q_all,
-    hub_acc, hub_in, contrib, runs, b_send, b_recv, fg_out,
+    hub_acc, hub_in, contrib, runs, b_send, b_recv, fg_out, order_v, order,
     h_src, h_rx, h_zsrc, h_rz, h_zg, h_xg,
-    wg_src, wg_recv, wg_xsrc, wg_rx, wg_zsrc, wg_rz,
+    wg_src, wg_pair, wg_half, wg_recv, wg_xsrc, wg_rx, wg_zsrc, wg_rz,
     s_x, s_misc, s_adj, s_cot_own, s_out,
-    s_nbr, s_cot, s_y, s_q, s_act, s_back, s_hx, s_hz, s_hzg, s_hxg, s_wf, s_wx, s_wz,
+    s_nbr, s_cot, s_y, s_q, s_act, s_back, s_hx, s_hz, s_hzg, s_hxg, s_wp, s_wf, s_wx, s_wz,
 ):
     nx, nz, nf, nb, slots = sizes
+    far, z_first, z_near = groups
+    ny = nf // 2
     nd = nx * nz
     fl, vl = x.shape
     full = w.shape[0]
@@ -60,6 +62,7 @@
     dom = lax.axis_index("dom")
     me = lax.axis_index("feat")
     my_x, my_z = dom // nz, dom % nz
+    my_y, my_core = me // 2, me % 2
     nxt, prv = (dom + 1) % nd, (dom + nd - 1) % nd
 
     def feat_peer(k):
@@ -135,15 +138,21 @@
         greet(x_dev(k))
     loop(1, nz, lambda k: greet(z_dev(k)))
     loop(1, nf, lambda k: greet(f_dev(k)))
-    pl.semaphore_wait(barrier, 2 + (nx - 1) + (nz - 1) + (nf - 1))
-
     for copy in x_loads:
         copy.wait()
-    mine = ext.at[pl.ds(nb, nb)]
-    to_nxt = remote(mine, ext.at[pl.ds(0, nb)], s_nbr, 0, to(nxt, me))
-    to_prv = remote(mine, ext.at[pl.ds(2 * nb, nb)], s_nbr, 1, to(prv, me))
-    to_nxt.start()
-    to_prv.start()
+
+    half = nb // 2
+
+    def ext_copy(side, h):
+        at, device = ((0, to(nxt, me)), (2 * nb, to(prv, me)))[side]
+        return remote(
+            ext.at[pl.ds(nb + half * h, half)], ext.at[pl.ds(at + half * h, half)],
+            s_nbr.at[h], side, device,
+        )
+
+    def both_sides(copies, h):
+        copies(0, h).start()
+        copies(1, h).start()
 
     def cot_copy(k):
         p = feat_peer(k)
@@ -156,8 +165,14 @@
     hub_acc[...] = jnp.zeros_like(hub_acc)
 
     def own_hubs(p):
-        row = lax.broadcasted_iota(jnp.int32, (vw, nh), 0) + p * vw
-        chunk = jnp.where(row == local_id, 1.0, 0.0).astype(BF16)
+        row = lax.broadcasted_iota(jnp.int32, (vw, 128), 0) + p * vw
+        chunk = jnp.concatenate(
+            [
+                jnp.where(row == local_id[g : g + 1], 1.0, 0.0).astype(BF16)
+                for g in range(nh // 128)
+            ],
+            axis=1,
+        )
         pick[p] = chunk
         left = stacked(jnp.concatenate([ext[nb + pb * p + j] for j in range(pb)], axis=1))
         both = mm(left, chunk, NN)
@@ -165,71 +180,85 @@
 
     loop(0, nf, own_hubs)
 
-    def x_rs_copy(s, k):
-        return remote(h_src.at[s, x_peer(k)], h_rx.at[s, k - 1], s_hx.at[s], k - 1, x_dev(k))
+    pl.semaphore_wait(barrier, 2 + (nx - 1) + (nz - 1) + (nf - 1))
+
+    parts = ((0, far), (far, nz - far))
+    near = ((0, nz - far), (nz - far, far))
+    far_steps = ((z_first, z_first + far),)
+    near_steps = ((z_first + far, nz), (1, z_first))
+
+    def steps(ranges, body):
+        for lower, upper in ranges:
+            loop(lower, upper, body)
+
+    def x_rs_copy(s, k, h):
+        at = pl.ds(*parts[h])
+        return remote(
+            h_src.at[s, x_peer(k), at], h_rx.at[s, k - 1, at], s_hx.at[s, h], k - 1, x_dev(k)
+        )
 
     def z_rs_copy(s, k):
-        return remote(h_zsrc.at[s, z_peer(k)], h_rz.at[s, k - 1], s_hz.at[s], k - 1, z_dev(k))
+        src = h_zsrc.at[s, (k + nz - z_first) % nz]
+        return remote(src, h_rz.at[s, k - 1], s_hz.at[s], k - 1, z_dev(k))
 
     def z_ag_copy(s, k):
-        return remote(h_zg.at[s, my_z], h_zg.at[s, my_z], s_hzg.at[s], k - 1, z_dev(k))
-
-    def z_ag_recv(s, k):
-        at = h_zg.at[s, z_from(k)]
-        return remote(at, at, s_hzg.at[s], k - 1, z_dev(k))
-
-    def x_ag_copy(s, k):
-        return remote(h_zg.at[s], h_xg.at[s, my_x], s_hxg.at[s], k - 1, x_dev(k))
-
-    def x_ag_recv(s, k):
-        return remote(
-            h_zg.at[s], h_xg.at[s, (my_x + nx - k) % nx], s_hxg.at[s], k - 1, x_dev(k)
-        )
+        dst = h_zg.at[s, (z_near + nz - k) % nz]
+        return remote(h_zg.at[s, z_near], dst, s_hzg.at[s], k - 1, z_dev(k))
+
+    def x_ag_copy(s, k, h):
+        at = pl.ds(*near[h])
+        return remote(h_zg.at[s, at], h_xg.at[s, k, at], s_hxg.at[s, h], k - 1, x_dev(k))
+
+    x_order = [2, 1, 3][:nx] if nx > 2 else [1]
 
     def hub_start(s):
         for q in range(nx):
             for i in range(nz):
                 r, c = i // per_q, q * per_q + i % per_q
-                h_src[s, q, i] = hub_acc[8 * r : 8 * r + 8, 128 * c : 128 * c + 128]
-        for k in range(1, nx):
-            x_rs_copy(s, k).start()
+                at = (i + 2 * nz - my_z - z_first) % nz
+                h_src[s, q, at] = hub_acc[8 * r : 8 * r + 8, 128 * c : 128 * c + 128]
+        for h in range(2):
+            for k in x_order:
+                x_rs_copy(s, k, h).start()
 
     def hub_z(s):
-        for k in range(1, nx):
-            x_rs_copy(s, k).wait_recv()
-        total = h_src[s, my_x]
-        for k in range(1, nx):
-            total += h_rx[s, k - 1]
-        h_zsrc[s] = total
-        loop(1, nz, lambda k: z_rs_copy(s, k).start())
+        for h in range(2):
+            for k in x_order:
+                x_rs_copy(s, k, h).wait_recv()
+            at = pl.ds(*parts[h])
+            total = h_src[s, my_x, at]
+            for k in range(1, nx):
+                total += h_rx[s, k - 1, at]
+            h_zsrc[s, at] = total
+            steps((far_steps, near_steps)[h], lambda k: z_rs_copy(s, k).start())
 
     def hub_zg(s):
         loop(1, nz, lambda k: z_rs_copy(s, k).wait_recv())
-        total = h_zsrc[s, my_z]
+        total = h_zsrc[s, nz - z_first]
         for k in range(1, nz):
             total += h_rz[s, k - 1]
-        h_zg[s, my_z] = total
-        loop(1, nz, lambda k: z_ag_copy(s, k).start())
-
-    def hub_xg(s):
-        loop(1, nz, lambda k: z_ag_recv(s, k).wait_recv())
-        for k in range(1, nx):
-            x_ag_copy(s, k).start()
-        h_xg[s, my_x] = h_zg[s]
+        h_zg[s, z_near] = total
+        steps(far_steps + near_steps, lambda k: z_ag_copy(s, k).start())
+
+    def hub_xg(s, h):
+        steps((near_steps, far_steps)[h], lambda k: z_ag_copy(s, k).wait_recv())
+        for k in x_order:
+            x_ag_copy(s, k, h).start()
+        at = pl.ds(*near[h])
+        h_xg[s, 0, at] = h_zg[s, at]
 
     def hub_end(s):
-        for k in range(1, nx):
-            x_ag_recv(s, k).wait_recv()
+        for h in range(2):
+            for k in x_order:
+                x_ag_copy(s, k, h).wait_recv()
         for q in range(nx):
             for i in range(nz):
                 r, c = i // per_q, q * per_q + i % per_q
-                high, low = split(h_xg[s, q, i])
-                hub_acc[8 * r : 8 * r + 8, 128 * c : 128 * c + 128] = h_xg[s, q, i]
+                tile = h_xg[s, (my_x + nx - q) % nx, (i + nz - my_z + z_near) % nz]
+                hub_acc[8 * r : 8 * r + 8, 128 * c : 128 * c + 128] = tile
         hub_in[...] = stacked(hub_acc[...])
 
     hub_start(0)
-    loop(1, nf, lambda k: cot_copy(k).start())
-
     tiles_load.wait()
 
     def split_tiles(b):
@@ -239,6 +268,47 @@
 
     loop(0, nb, split_tiles)
     hub_z(0)
+    both_sides(ext_copy, 0)
+    loop(1, nf, lambda k: cot_copy(k).start())
+
+    entries = nb * slots
+    none = 3 * nb
+    row = lax.broadcasted_iota(jnp.int32, (nb, slots), 0)
+    lane = lax.broadcasted_iota(jnp.int32, (nb, slots), 1)
+    place = row * slots + lane
+    counts = jnp.zeros((nb, slots), jnp.int32)
+    for b in range(nb):
+        counts = jnp.where(row == b, count[b], counts)
+    target = jnp.where(lane < counts, cols_v[...], none)
+    along = lax.broadcasted_iota(jnp.int32, (1, 128), 1)
+
+    def one(flag):
+        return jnp.where(flag, 1, 0)
+
+    def rank_step(e, carry):
+        rank, again, upto, found = carry
+        b, k = e // slots, e % slots
+        goal = jnp.where(k < count[b], cols[b, k], none)
+        tie = one(target == goal) * one(place > e)
+        return (
+            rank + one(target > goal) + tie, jnp.maximum(again, tie),
+            upto + one(along >= goal), jnp.maximum(found, one(along == goal)),
+        )
+
+    zero, zeros = jnp.zeros((nb, slots), jnp.int32), jnp.zeros((1, 128), jnp.int32)
+    rank, again, upto, found = lax.fori_loop(0, entries, rank_step, (zero, zero, zeros, zeros))
+    which, same = zeros, zeros
+    for e in range(entries):
+        b, k = e // slots, e % slots
+        here = rank[b : b + 1, k : k + 1] == along
+        which = jnp.where(here, e, which)
+        same = jnp.where(here, again[b : b + 1, k : k + 1], same)
+    order_v[0:1] = which
+    order_v[1:2] = same
+    order_v[2:3] = jnp.maximum(upto - 1, 0)
+    order_v[3:4] = found
+    order_copy = pltpu.make_async_copy(order_v, order, s_misc.at[2])
+    order_copy.start()
 
     w_load.wait()
     w_st[...] = stacked(w_f32[...])
@@ -253,17 +323,22 @@
         copy.wait()
     loop(0, nf // 2, split_adj)
     hub_zg(0)
+    both_sides(ext_copy, 1)
     loop(nf // 2, nf, split_adj)
-    hub_xg(0)
-
-    to_nxt.wait_recv()
-    to_prv.wait_recv()
+    order_copy.wait()
+    hub_xg(0, 0)
+    hub_xg(0, 1)
+
+    for h in range(2):
+        ext_copy(0, h).wait_recv()
+        ext_copy(1, h).wait_recv()
 
     def tile_part(p):
         for j in range(pb):
             b = p * pb + j
             left = jnp.concatenate(
-                [ext[cols[b * slots + k]] * live[b * slots + k] for k in range(slots)], axis=1
+                [ext[cols[b, k]] * jnp.where(k < count[b], 1.0, 0.0) for k in range(slots)],
+                axis=1,
             )
             y_send[p, :, 128 * j : 128 * j + 128] = mm3(stacked(left), cat_hi[b], cat_lo[b], NT)
 
@@ -283,12 +358,16 @@
     def hub_to_y(p):
         return y_send[p] + mm3(hub_in[...], adj_hi[p], adj_lo[p], NN)
 
-    def hub_part(k):
+    def feat_order(i):
+        return nf // 2 if nf < 4 else (nf // 2 + (1 - 2 * (i % 2)) * ((i + 1) // 2)) % nf
+
+    def hub_part(i):
+        k = feat_order(i)
         p = feat_peer(k)
         y_send[p] = hub_to_y(p)
         y_copy(k).start()
 
-    loop(1, nf, hub_part)
+    loop(0, nf - 1, hub_part)
     y_all[pl.ds(pl.multiple_of(fl * me, 8), fl), :] = hub_to_y(me)
 
     loop(1, nf, lambda k: y_recv(k).wait_recv())
@@ -316,18 +395,19 @@
     def q_recv(k):
         return remote(rows_of(q_send, me), q_all.at[feat_from(k)], s_q, k - 1, f_dev(k))
 
-    loop(1, nf, lambda k: q_copy(k).start())
+    loop(0, nf - 1, lambda i: q_copy(feat_order(i)).start())
     q_all[me] = q_send[pl.ds(pl.multiple_of(fl * me, 8), fl), :]
 
     g_st = jnp.concatenate([g_hi, g_lo], axis=0)
     terms = mm3(g_st, y_hi, y_lo, NT)
     for p in range(nf):
-        wg_src[p] = terms[fl * p : fl * p + fl]
+        wg_src[p % 2, p // 2] = terms[fl * p : fl * p + fl]
+    pair = remote(wg_src.at[1 - my_core], wg_pair, s_wp, 0, to(dom, me + 1 - 2 * my_core))
+    pair.start()
 
     def wf_copy(k):
-        return remote(wg_src.at[feat_peer(k)], wg_recv.at[k - 1], s_wf, k - 1, f_dev(k))
-
-    loop(1, nf, lambda k: wf_copy(k).start())
+        y = (my_y + k) % ny
+        return remote(wg_half.at[y], wg_recv.at[k - 1], s_wf, k - 1, to(dom, y * 2 + my_core))
 
     def act_at(p):
         return act.at[:, pl.ds(pl.multiple_of(vw * p, 128), vw)]
@@ -338,8 +418,8 @@
     def act_recv(k):
         return remote(rows_of(act_send, me), act_at(feat_from(k)), s_act, k - 1, f_dev(k))
 
-    loop(1, nf, lambda k: act_copy(k).start())
-    act_own = pltpu.make_async_copy(rows_of(act_send, me), act_at(me), s_misc.at[2])
+    loop(0, nf - 1, lambda i: act_copy(feat_order(i)).start())
+    act_own = pltpu.make_async_copy(rows_of(act_send, me), act_at(me), s_misc.at[3])
     act_own.start()
 
     def hub_back(p):
@@ -354,6 +434,10 @@
 
     loop(1, nf, hub_step)
     hub_start(1)
+    pair.wait_recv()
+    wg_half[...] = wg_src[my_core] + wg_pair[...]
+    for k in [2, 1, 3] if ny > 2 else []:
+        wf_copy(k).start()
 
     def slot_terms(p):
         for j in range(pb):
@@ -366,28 +450,34 @@
     loop(0, nf, slot_terms)
 
     def run_step(j, total):
-        total = total * keep[j] + contrib[ent[j]]
+        total = total * order[1, j].astype(F32) + contrib[order[0, j]]
         runs[j] = total
         return total
 
     lax.fori_loop(0, nb * slots, run_step, jnp.zeros((fl, 128), F32))
 
+    def summed(block):
+        return runs[order[2, block]] * order[3, block].astype(F32)
+
     def back_send(b):
-        b_send[0, b] = runs[last[b]] * has[b]
-        b_send[1, b] = runs[last[2 * nb + b]] * has[2 * nb + b]
+        b_send[0, b] = summed(b)
+        b_send[1, b] = summed(2 * nb + b)
 
     loop(0, nb, back_send)
-    back_prv = remote(b_send.at[0], b_recv.at[0], s_back, 0, to(prv, me))
-    back_nxt = remote(b_send.at[1], b_recv.at[1], s_back, 1, to(nxt, me))
-    back_prv.start()
-    back_nxt.start()
+
+    def back_copy(side, h):
+        at = pl.ds(half * h, half)
+        device = (to(prv, me), to(nxt, me))[side]
+        return remote(b_send.at[side, at], b_recv.at[side, at], s_back.at[h], side, device)
 
     hub_z(1)
+    both_sides(back_copy, 0)
     hub_zg(1)
-
-    loop(1, nf, lambda k: wf_copy(k).wait_recv())
-    term = wg_src[me]
-    for k in range(1, nf):
+    both_sides(back_copy, 1)
+
+    term = wg_half[my_y]
+    for k in range(1, ny):
+        wf_copy(k).wait_recv()
         term += wg_recv[k - 1]
     part = full // nx
     for q in range(nx):
@@ -399,7 +489,7 @@
     for k in range(1, nx):
         wx_copy(k).start()
 
-    hub_xg(1)
+    hub_xg(1, 0)
 
     for k in range(1, nx):
         wx_copy(k).wait_recv()
@@ -416,10 +506,12 @@
         return remote(wg_zsrc.at[z_peer(k)], wg_rz.at[k - 1], s_wz, k - 1, z_dev(k))
 
     loop(1, nz, lambda k: wz_copy(k).start())
+    hub_xg(1, 1)
 
     hub_end(1)
-    back_prv.wait_recv()
-    back_nxt.wait_recv()
+    for h in range(2):
+        back_copy(0, h).wait_recv()
+        back_copy(1, h).wait_recv()
 
     def out_copy(p):
         return pltpu.make_async_copy(
@@ -431,7 +523,7 @@
         placed = both[:fl] + both[fl:]
         for j in range(pb):
             b = p * pb + j
-            own = runs[last[nb + b]] * has[nb + b]
+            own = summed(nb + b)
             total = placed[:, 128 * j : 128 * j + 128] + own + b_recv[0, b] + b_recv[1, b]
             fg_out[p, :, 128 * j : 128 * j + 128] = total
         out_copy(p).start()
@@ -446,23 +538,26 @@
 
     act_own.wait()
     loop(1, nf, lambda k: act_recv(k).wait_recv())
-    to_nxt.wait_send()
-    to_prv.wait_send()
-    back_prv.wait_send()
-    back_nxt.wait_send()
+    pair.wait_send()
+    for h in range(2):
+        for side in range(2):
+            ext_copy(side, h).wait_send()
+            back_copy(side, h).wait_send()
+    for k in range(1, ny):
+        wf_copy(k).wait_send()
 
     def feat_sent(k):
         cot_copy(k).wait_send()
         y_copy(k).wait_send()
         q_copy(k).wait_send()
-        wf_copy(k).wait_send()
         act_copy(k).wait_send()
 
     loop(1, nf, feat_sent)
     for k in range(1, nx):
         for s in range(2):
-            x_rs_copy(s, k).wait_send()
-            x_ag_copy(s, k).wait_send()
+            for h in range(2):
+                x_rs_copy(s, k, h).wait_send()
+                x_ag_copy(s, k, h).wait_send()
         wx_copy(k).wait_send()
 
     def z_sent(k):
@@ -473,6 +568,34 @@
 
     loop(1, nz, z_sent)
     loop(0, nf, lambda p: out_copy(p).wait())
+
+
+def hand_over_kernel(count, *refs):
+    ins, outs = refs[:count], refs[count : 2 * count]
+    held, sems = refs[2 * count : 3 * count], refs[-1]
+    reads = [pltpu.make_async_copy(ins[i], held[i], sems.at[0, i]) for i in range(count)]
+    writes = [pltpu.make_async_copy(held[i], outs[i], sems.at[1, i]) for i in range(count)]
+    for read in reads:
+        read.start()
+    for read, write in zip(reads, writes):
+        read.wait()
+        write.start()
+    for write in writes:
+        write.wait()
+
+
+def hand_over(arrays):
+    hbm = pl.BlockSpec(memory_space=pl.ANY)
+    count = len(arrays)
+    return pl.pallas_call(
+        functools.partial(hand_over_kernel, count),
+        out_shape=tuple(jax.ShapeDtypeStruct(a.shape, a.dtype) for a in arrays),
+        in_specs=[hbm] * count,
+        out_specs=(hbm,) * count,
+        scratch_shapes=[pltpu.VMEM(a.shape, a.dtype) for a in arrays]
+        + [pltpu.SemaphoreType.DMA((2, count))],
+        compiler_params=pltpu.CompilerParams(vmem_limit_bytes=60 * 1024 * 1024),
+    )(*arrays)
 
 
 def local(nd, nf, nx, node_feats, weight, tiles, block_cols, block_count, hub_ids, hub_adj, cotangent):
@@ -483,23 +606,10 @@
     nh = hub_adj.shape[0]
     vw = vl // nf
     entries = nb * slots
-
-    col = block_cols.reshape(-1)
-    alive = (jnp.arange(slots, dtype=jnp.int32)[None, :] < block_count[:, None]).reshape(-1)
-    target = jnp.where(alive, col, 3 * nb)
-    at = jnp.arange(entries, dtype=jnp.int32)
-    before = target[None, :] * entries + at[None, :] < target[:, None] * entries + at[:, None]
-    rank = jnp.sum(before.astype(jnp.int32), axis=1)
-    placed = rank[:, None] == at[None, :]
-    ent = jnp.sum(jnp.where(placed, at[:, None], 0), axis=0)
-    repeat = jnp.any((target[None, :] == target[:, None]) & (at[None, :] < at[:, None]), axis=1)
-    keep = jnp.sum(jnp.where(placed & repeat[:, None], 1.0, 0.0), axis=0)
-    blocks = jnp.arange(3 * nb, dtype=jnp.int32)
-    upto = jnp.sum((target[:, None] <= blocks[None, :]).astype(jnp.int32), axis=0)
-    last = jnp.maximum(upto - 1, 0)
-    has = jnp.any(target[:, None] == blocks[None, :], axis=0).astype(F32)
-    live = alive.astype(F32)
-
+    ny = nf // 2
+    far = 7 if nz == 16 else 1
+    z_near = (nz - far) // 2
+    groups = (far, z_near + 1, z_near)
     lanes = max(fl, 128)
     vm = pltpu.VMEM
     dma = pltpu.SemaphoreType.DMA
@@ -516,38 +626,41 @@
         vm((fl, nh), F32), vm((2 * fl, nh), BF16),
         vm((entries, fl, 128), F32), vm((entries, fl, 128), F32),
         vm((2, nb, fl, 128), F32), vm((2, nb, fl, 128), F32), vm((nf, fl, vw), F32),
+        vm((8, 128), jnp.int32), pltpu.SMEM((8, 128), jnp.int32),
         vm((2, nx, nz) + hub_tile, F32), vm((2, nx - 1, nz) + hub_tile, F32),
         vm((2, nz) + hub_tile, F32), vm((2, nz - 1) + hub_tile, F32),
         vm((2, nz) + hub_tile, F32), vm((2, nx, nz) + hub_tile, F32),
-        vm((nf, fl, full), F32), vm((nf - 1, fl, full), F32),
+        vm((2, ny, fl, full), F32), vm((ny, fl, full), F32), vm((ny, fl, full), F32),
+        vm((max(ny - 1, 1), fl, full), F32),
         vm((nx, fl, full // nx), F32), vm((nx - 1, fl, full // nx), F32),
         vm((nz, full // nx // nz, lanes), F32), vm((nz - 1, full // nx // nz, lanes), F32),
-        dma((nb,)), dma((3,)), dma((nf,)), dma, dma((nf,)),
-        dma((2, 2)), dma((2, nf - 1)), dma((2, nf - 1)), dma((2, nf - 1)), dma((2, nf - 1)),
-        dma((2, 2)),
-        dma((2, 2, nx - 1)), dma((2, 2, nz - 1)), dma((2, 2, nz - 1)), dma((2, 2, nx - 1)),
-        dma((2, nf - 1)), dma((2, nx - 1)), dma((2, nz - 1)),
+        dma((nb,)), dma((4,)), dma((nf,)), dma, dma((nf,)),
+        dma((2, 2, 2)), dma((2, nf - 1)), dma((2, nf - 1)), dma((2, nf - 1)), dma((2, nf - 1)),
+        dma((2, 2, 2)),
+        dma((2, 2, 2, nx - 1)), dma((2, 2, nz - 1)), dma((2, 2, nz - 1)), dma((2, 2, 2, nx - 1)),
+        dma((2, 1)), dma((2, max(ny - 1, 1))), dma((2, nx - 1)), dma((2, nz - 1)),
     ]
     hbm = pl.BlockSpec(memory_space=pl.ANY)
     vmem = pl.BlockSpec(memory_space=pltpu.VMEM)
     smem = pl.BlockSpec(memory_space=pltpu.SMEM)
-    return pl.pallas_call(
-        functools.partial(kernel, (nx, nz, nf, nb, slots)),
+    results = pl.pallas_call(
+        functools.partial(kernel, (nx, nz, nf, nb, slots), groups),
         out_shape=(
             jax.ShapeDtypeStruct((fl, vl), F32),
             jax.ShapeDtypeStruct((fl, vl), F32),
             jax.ShapeDtypeStruct((full // nd, fl), F32),
         ),
-        in_specs=[hbm] * 5 + [vmem] + [smem] * 6,
+        in_specs=[hbm] * 5 + [vmem] * 2 + [smem] * 2,
         out_specs=(hbm, hbm, vmem),
         scratch_shapes=scratch,
         compiler_params=pltpu.CompilerParams(
             collective_id=0, has_side_effects=True, vmem_limit_bytes=60 * 1024 * 1024
         ),
     )(
-        node_feats, weight, tiles, hub_adj, cotangent, hub_ids.reshape(1, nh),
-        col, live, ent, keep, last, has,
+        node_feats, weight, tiles, hub_adj, cotangent, hub_ids.reshape(nh // 128, 128),
+        block_cols, block_cols, block_count,
     )
+    return hand_over(results)
 
 
 def solution(mesh):

time: 125 us -> 101 us (0.81)
  the two profiles are of different devices: /device:TPU:1 before, /device:TPU:25 now
where the time goes in v2:
time: 101 us
  Pallas kernels  99.2 us (98%)
  local copies, waits for them, and re-layouts  1.36 us (1%)
    pallas_call x1, Pallas kernels, local(): pl.pallas_call(functools.partial(kernel, (nx, nz, nf, nb, slots), groups)...  97.1 us
    pallas_call x1, Pallas kernels, hand_over(): pl.pallas_call(functools.partial(hand_over_kernel, count), out_shape=tupl...  2.06 us

profile of v2, /device:TPU:25, one launch (start us, length us, event | category | flops | bytes accessed | tf_op | source)
XLA Modules:
  0.0 101.2 jit_solution(5760174497064490502)
XLA Ops:
  0.6 1.4 %copy.11.cols_v.cols = s32[16,4]{1,0:T(8,128)} copy(s32[16,4]{0,1:T(4,128)} %param.11) | data formatting | bytes 512 | tf_op args[3]
  2.0 97.1 %shard_map.103 = (f32[64,2048]{1,0:T(8,128)}, f32[64,2048]{1,0:T(8,128)}, f32[8,64]{1,0:T(8,128)}) custom-call(f32[64,2048]{1,0:T(8,128)} %x.1, f32[512,512]{1,0:T(8,128)} %w.1, f32[16,4,128,128]{3,2,1,0:T(8,128)} %tiles.1, f32[1024,2048]{1,0:T(8,128)} %hub_adj.1, f32[64,2048]{1,0:T(8,128)} %cot.1, s32[8,128]{1,0:T(8,128)} %bitcast.1, ...), custom_call_target="tpu_custom_call" | custom-call | tf_op jit(solution)/shard_map/pallas_call | solution.py:646
  99.1 2.1 %shard_map.104 = (f32[64,2048]{1,0:T(8,128)}, f32[64,2048]{1,0:T(8,128)}, f32[8,64]{1,0:T(8,128)}) custom-call(f32[64,2048]{1,0:T(8,128)} %get-tuple-element.6.refs_0_, f32[64,2048]{1,0:T(8,128)} %get-tuple-element.7.refs_1_, f32[8,64]{1,0:T(8,128)} %get-tuple-element.8.refs_2_), custom_call_target="tpu_custom_call" | custom-call | tf_op jit(solution)/shard_map/pallas_call | solution.py:590

commit v3 on v2

--- a/solution.py
+++ b/solution.py
@@ -37,7 +37,7 @@
 
 
 def kernel(
-    sizes, groups,
+    sizes,
     x, w, tiles, hub_adj, cot, ids, cols_v, cols, count,
     act, fg, wg,
     ext, adj_f32, adj_hi, adj_lo, tiles_f32, cat_hi, cat_lo, pick,
@@ -49,7 +49,6 @@
     s_nbr, s_cot, s_y, s_q, s_act, s_back, s_hx, s_hz, s_hzg, s_hxg, s_wp, s_wf, s_wx, s_wz,
 ):
     nx, nz, nf, nb, slots = sizes
-    far, z_first, z_near = groups
     ny = nf // 2
     nd = nx * nz
     fl, vl = x.shape
@@ -77,8 +76,11 @@
     def z_peer(k):
         return (my_z + k) % nz
 
-    def z_from(k):
-        return (my_z + nz - k) % nz
+    def z_step(o):
+        return (nz // 2 + (1 - 2 * (o % 2)) * ((o + 1) // 2) + nz) % nz
+
+    def z_back(o):
+        return o + (2 * (o % 2) - 1) * ((o + nz - 1) // nz)
 
     def to(domain, feature):
         return {"dom": domain, "feat": feature}
@@ -105,6 +107,17 @@
 
         lax.fori_loop(lower, upper, step, 0)
 
+    barrier = pltpu.get_barrier_semaphore()
+
+    def greet(device):
+        pl.semaphore_signal(barrier, inc=1, device_id=device, device_id_type=MESH)
+
+    loop(0, nz - 1, lambda o: greet(z_dev(z_step(o))))
+    for k in range(1, nx):
+        greet(x_dev(k))
+    greet(to(nxt, me))
+    greet(to(prv, me))
+    loop(1, nf, lambda k: greet(f_dev(k)))
     x_loads = [
         pltpu.make_async_copy(x.at[:, pl.ds(128 * b, 128)], ext.at[nb + b], s_x.at[b])
         for b in range(nb)
@@ -127,17 +140,6 @@
     for copy in adj_loads:
         copy.start()
 
-    barrier = pltpu.get_barrier_semaphore()
-
-    def greet(device):
-        pl.semaphore_signal(barrier, inc=1, device_id=device, device_id_type=MESH)
-
-    greet(to(nxt, me))
-    greet(to(prv, me))
-    for k in range(1, nx):
-        greet(x_dev(k))
-    loop(1, nz, lambda k: greet(z_dev(k)))
-    loop(1, nf, lambda k: greet(f_dev(k)))
     for copy in x_loads:
         copy.wait()
 
@@ -182,79 +184,86 @@
 
     pl.semaphore_wait(barrier, 2 + (nx - 1) + (nz - 1) + (nf - 1))
 
-    parts = ((0, far), (far, nz - far))
-    near = ((0, nz - far), (nz - far, far))
-    far_steps = ((z_first, z_first + far),)
-    near_steps = ((z_first + far, nz), (1, z_first))
-
-    def steps(ranges, body):
-        for lower, upper in ranges:
-            loop(lower, upper, body)
+    cuts = (0, 3, 9, nz) if nz == 16 else (0, 1, nz)
+    pieces = [(cuts[i], cuts[i + 1]) for i in range(len(cuts) - 1)]
+    own_at = nz - 1
+
+    def piece(h):
+        lower, upper = pieces[h]
+        return pl.ds(lower, upper - lower)
+
+    def z_loop(h, body):
+        lower, upper = pieces[h]
+        loop(lower, min(upper, nz - 1), body)
 
     def x_rs_copy(s, k, h):
-        at = pl.ds(*parts[h])
+        at = piece(h)
         return remote(
             h_src.at[s, x_peer(k), at], h_rx.at[s, k - 1, at], s_hx.at[s, h], k - 1, x_dev(k)
         )
 
-    def z_rs_copy(s, k):
-        src = h_zsrc.at[s, (k + nz - z_first) % nz]
-        return remote(src, h_rz.at[s, k - 1], s_hz.at[s], k - 1, z_dev(k))
-
-    def z_ag_copy(s, k):
-        dst = h_zg.at[s, (z_near + nz - k) % nz]
-        return remote(h_zg.at[s, z_near], dst, s_hzg.at[s], k - 1, z_dev(k))
+    def z_rs_copy(s, o):
+        return remote(h_zsrc.at[s, o], h_rz.at[s, o], s_hz.at[s], o, z_dev(z_step(o)))
+
+    def z_ag_copy(s, o):
+        dst = h_zg.at[s, z_back(o)]
+        return remote(h_zg.at[s, own_at], dst, s_hzg.at[s], o, z_dev(z_step(o)))
 
     def x_ag_copy(s, k, h):
-        at = pl.ds(*near[h])
+        at = piece(h)
         return remote(h_zg.at[s, at], h_xg.at[s, k, at], s_hxg.at[s, h], k - 1, x_dev(k))
 
     x_order = [2, 1, 3][:nx] if nx > 2 else [1]
+
+    def z_place(i):
+        step = (i + nz - my_z) % nz
+        down = 2 * (nz // 2 - step) - 1
+        up = 2 * (step - nz // 2)
+        return jnp.where(step < nz // 2, down, up)
 
     def hub_start(s):
         for q in range(nx):
             for i in range(nz):
                 r, c = i // per_q, q * per_q + i % per_q
-                at = (i + 2 * nz - my_z - z_first) % nz
-                h_src[s, q, at] = hub_acc[8 * r : 8 * r + 8, 128 * c : 128 * c + 128]
-        for h in range(2):
+                h_src[s, q, z_place(i)] = hub_acc[8 * r : 8 * r + 8, 128 * c : 128 * c + 128]
+        for h in range(len(pieces)):
             for k in x_order:
                 x_rs_copy(s, k, h).start()
 
     def hub_z(s):
-        for h in range(2):
+        for h in range(len(pieces)):
             for k in x_order:
                 x_rs_copy(s, k, h).wait_recv()
-            at = pl.ds(*parts[h])
+            at = piece(h)
             total = h_src[s, my_x, at]
             for k in range(1, nx):
                 total += h_rx[s, k - 1, at]
             h_zsrc[s, at] = total
-            steps((far_steps, near_steps)[h], lambda k: z_rs_copy(s, k).start())
+            z_loop(h, lambda o: z_rs_copy(s, o).start())
 
     def hub_zg(s):
-        loop(1, nz, lambda k: z_rs_copy(s, k).wait_recv())
-        total = h_zsrc[s, nz - z_first]
-        for k in range(1, nz):
-            total += h_rz[s, k - 1]
-        h_zg[s, z_near] = total
-        steps(far_steps + near_steps, lambda k: z_ag_copy(s, k).start())
+        loop(0, nz - 1, lambda o: z_rs_copy(s, o).wait_recv())
+        total = h_zsrc[s, own_at]
+        for o in range(nz - 1):
+            total += h_rz[s, o]
+        h_zg[s, own_at] = total
+        loop(0, nz - 1, lambda o: z_ag_copy(s, o).start())
 
     def hub_xg(s, h):
-        steps((near_steps, far_steps)[h], lambda k: z_ag_copy(s, k).wait_recv())
+        z_loop(h, lambda o: z_ag_copy(s, o).wait_recv())
         for k in x_order:
             x_ag_copy(s, k, h).start()
-        at = pl.ds(*near[h])
+        at = piece(h)
         h_xg[s, 0, at] = h_zg[s, at]
 
     def hub_end(s):
-        for h in range(2):
+        for h in reversed(range(len(pieces))):
             for k in x_order:
                 x_ag_copy(s, k, h).wait_recv()
         for q in range(nx):
             for i in range(nz):
                 r, c = i // per_q, q * per_q + i % per_q
-                tile = h_xg[s, (my_x + nx - q) % nx, (i + nz - my_z + z_near) % nz]
+                tile = h_xg[s, (my_x + nx - q) % nx, z_place(i)]
                 hub_acc[8 * r : 8 * r + 8, 128 * c : 128 * c + 128] = tile
         hub_in[...] = stacked(hub_acc[...])
 
@@ -273,13 +282,13 @@
 
     entries = nb * slots
     none = 3 * nb
-    row = lax.broadcasted_iota(jnp.int32, (nb, slots), 0)
-    lane = lax.broadcasted_iota(jnp.int32, (nb, slots), 1)
-    place = row * slots + lane
-    counts = jnp.zeros((nb, slots), jnp.int32)
+    row = lax.broadcasted_iota(jnp.int32, (slots, nb), 0)
+    lane = lax.broadcasted_iota(jnp.int32, (slots, nb), 1)
+    place = lane * slots + row
+    counts = jnp.zeros((slots, nb), jnp.int32)
     for b in range(nb):
-        counts = jnp.where(row == b, count[b], counts)
-    target = jnp.where(lane < counts, cols_v[...], none)
+        counts = jnp.where(lane == b, count[b], counts)
+    target = jnp.where(row < counts, cols_v[...], none)
     along = lax.broadcasted_iota(jnp.int32, (1, 128), 1)
 
     def one(flag):
@@ -288,21 +297,21 @@
     def rank_step(e, carry):
         rank, again, upto, found = carry
         b, k = e // slots, e % slots
-        goal = jnp.where(k < count[b], cols[b, k], none)
+        goal = jnp.where(k < count[b], cols[k, b], none)
         tie = one(target == goal) * one(place > e)
         return (
             rank + one(target > goal) + tie, jnp.maximum(again, tie),
             upto + one(along >= goal), jnp.maximum(found, one(along == goal)),
         )
 
-    zero, zeros = jnp.zeros((nb, slots), jnp.int32), jnp.zeros((1, 128), jnp.int32)
+    zero, zeros = jnp.zeros((slots, nb), jnp.int32), jnp.zeros((1, 128), jnp.int32)
     rank, again, upto, found = lax.fori_loop(0, entries, rank_step, (zero, zero, zeros, zeros))
     which, same = zeros, zeros
     for e in range(entries):
         b, k = e // slots, e % slots
-        here = rank[b : b + 1, k : k + 1] == along
+        here = rank[k : k + 1, b : b + 1] == along
         which = jnp.where(here, e, which)
-        same = jnp.where(here, again[b : b + 1, k : k + 1], same)
+        same = jnp.where(here, again[k : k + 1, b : b + 1], same)
     order_v[0:1] = which
     order_v[1:2] = same
     order_v[2:3] = jnp.maximum(upto - 1, 0)
@@ -326,8 +335,8 @@
     both_sides(ext_copy, 1)
     loop(nf // 2, nf, split_adj)
     order_copy.wait()
-    hub_xg(0, 0)
-    hub_xg(0, 1)
+    for h in reversed(range(len(pieces))):
+        hub_xg(0, h)
 
     for h in range(2):
         ext_copy(0, h).wait_recv()
@@ -337,7 +346,7 @@
         for j in range(pb):
             b = p * pb + j
             left = jnp.concatenate(
-                [ext[cols[b, k]] * jnp.where(k < count[b], 1.0, 0.0) for k in range(slots)],
+                [ext[cols[k, b]] * jnp.where(k < count[b], 1.0, 0.0) for k in range(slots)],
                 axis=1,
             )
             y_send[p, :, 128 * j : 128 * j + 128] = mm3(stacked(left), cat_hi[b], cat_lo[b], NT)
@@ -418,7 +427,6 @@
     def act_recv(k):
         return remote(rows_of(act_send, me), act_at(feat_from(k)), s_act, k - 1, f_dev(k))
 
-    loop(0, nf - 1, lambda i: act_copy(feat_order(i)).start())
     act_own = pltpu.make_async_copy(rows_of(act_send, me), act_at(me), s_misc.at[3])
     act_own.start()
 
@@ -472,8 +480,6 @@
 
     hub_z(1)
     both_sides(back_copy, 0)
-    hub_zg(1)
-    both_sides(back_copy, 1)
 
     term = wg_half[my_y]
     for k in range(1, ny):
@@ -489,7 +495,9 @@
     for k in range(1, nx):
         wx_copy(k).start()
 
-    hub_xg(1, 0)
+    hub_zg(1)
+    both_sides(back_copy, 1)
+    loop(0, nf - 1, lambda i: act_copy(feat_order(i)).start())
 
     for k in range(1, nx):
         wx_copy(k).wait_recv()
@@ -506,7 +514,10 @@
         return remote(wg_zsrc.at[z_peer(k)], wg_rz.at[k - 1], s_wz, k - 1, z_dev(k))
 
     loop(1, nz, lambda k: wz_copy(k).start())
-    hub_xg(1, 1)
+
+    for h in reversed(range(len(pieces))):
+        hub_xg(1, h)
+
 
     hub_end(1)
     for h in range(2):
@@ -555,18 +566,18 @@
     loop(1, nf, feat_sent)
     for k in range(1, nx):
         for s in range(2):
-            for h in range(2):
+            for h in range(len(pieces)):
                 x_rs_copy(s, k, h).wait_send()
                 x_ag_copy(s, k, h).wait_send()
         wx_copy(k).wait_send()
 
-    def z_sent(k):
+    def z_sent(o):
         for s in range(2):
-            z_rs_copy(s, k).wait_send()
-            z_ag_copy(s, k).wait_send()
-        wz_copy(k).wait_send()
-
-    loop(1, nz, z_sent)
+            z_rs_copy(s, o).wait_send()
+            z_ag_copy(s, o).wait_send()
+        wz_copy(o + 1).wait_send()
+
+    loop(0, nz - 1, z_sent)
     loop(0, nf, lambda p: out_copy(p).wait())
 
 
@@ -607,9 +618,6 @@
     vw = vl // nf
     entries = nb * slots
     ny = nf // 2
-    far = 7 if nz == 16 else 1
-    z_near = (nz - far) // 2
-    groups = (far, z_near + 1, z_near)
     lanes = max(fl, 128)
     vm = pltpu.VMEM
     dma = pltpu.SemaphoreType.DMA
@@ -637,14 +645,14 @@
         dma((nb,)), dma((4,)), dma((nf,)), dma, dma((nf,)),
         dma((2, 2, 2)), dma((2, nf - 1)), dma((2, nf - 1)), dma((2, nf - 1)), dma((2, nf - 1)),
         dma((2, 2, 2)),
-        dma((2, 2, 2, nx - 1)), dma((2, 2, nz - 1)), dma((2, 2, nz - 1)), dma((2, 2, 2, nx - 1)),
+        dma((2, 3, 2, nx - 1)), dma((2, 2, nz - 1)), dma((2, 2, nz - 1)), dma((2, 3, 2, nx - 1)),
         dma((2, 1)), dma((2, max(ny - 1, 1))), dma((2, nx - 1)), dma((2, nz - 1)),
     ]
     hbm = pl.BlockSpec(memory_space=pl.ANY)
     vmem = pl.BlockSpec(memory_space=pltpu.VMEM)
     smem = pl.BlockSpec(memory_space=pltpu.SMEM)
     results = pl.pallas_call(
-        functools.partial(kernel, (nx, nz, nf, nb, slots), groups),
+        functools.partial(kernel, (nx, nz, nf, nb, slots)),
         out_shape=(
             jax.ShapeDtypeStruct((fl, vl), F32),
             jax.ShapeDtypeStruct((fl, vl), F32),
@@ -658,7 +666,7 @@
         ),
     )(
         node_feats, weight, tiles, hub_adj, cotangent, hub_ids.reshape(nh // 128, 128),
-        block_cols, block_cols, block_count,
+        block_cols.T, block_cols.T, block_count,
     )
     return hand_over(results)
 

time: 101 us -> 97.7 us (0.967)
  the two profiles are of different devices: /device:TPU:25 before, /device:TPU:1 now
where the time goes in v3:
time: 97.7 us; the launch traced here: 96.8 us
  Pallas kernels  96.2 us (98%)
    pallas_call x1, Pallas kernels, local(): pl.pallas_call(functools.partial(kernel, (nx, nz, nf, nb, slots)), out_sh...  94.1 us
    pallas_call x1, Pallas kernels, hand_over(): pl.pallas_call(functools.partial(hand_over_kernel, count), out_shape=tupl...  2.06 us

profile of v3, /device:TPU:1, one launch (start us, length us, event | category | flops | bytes accessed | tf_op | source)
XLA Modules:
  0.0 96.8 jit_solution(16426757052097965894)
XLA Ops:
  0.6 94.1 %shard_map.103 = (f32[64,2048]{1,0:T(8,128)}, f32[64,2048]{1,0:T(8,128)}, f32[8,64]{1,0:T(8,128)}) custom-call(f32[64,2048]{1,0:T(8,128)} %x.1, f32[512,512]{1,0:T(8,128)} %w.1, f32[16,4,128,128]{3,2,1,0:T(8,128)} %tiles.1, f32[1024,2048]{1,0:T(8,128)} %hub_adj.1, f32[64,2048]{1,0:T(8,128)} %cot.1, s32[8,128]{1,0:T(8,128)} %bitcast.4, s32[4,16]{1,0:T(4,128)} %bitcast.2, ...), custom_call_target="tpu_custom_call" | custom-call | tf_op jit(solution)/shard_map/pallas_call | solution.py:654
  94.7 2.1 %shard_map.104 = (f32[64,2048]{1,0:T(8,128)}, f32[64,2048]{1,0:T(8,128)}, f32[8,64]{1,0:T(8,128)}) custom-call(f32[64,2048]{1,0:T(8,128)} %get-tuple-element.6.refs_0_, f32[64,2048]{1,0:T(8,128)} %get-tuple-element.7.refs_1_, f32[8,64]{1,0:T(8,128)} %get-tuple-element.8.refs_2_), custom_call_target="tpu_custom_call" | custom-call | tf_op jit(solution)/shard_map/pallas_call | solution.py:601

commit v4 on v3

--- a/solution.py
+++ b/solution.py
@@ -13,6 +13,8 @@
 BF16 = jnp.bfloat16
 NN = (((1,), (0,)), ((), ()))
 NT = (((1,), (1,)), ((), ()))
+THERE = ((), (0, 1), (2, 3))
+BACK = ((), (0, 1), (2, 3))
 
 
 def split(value):
@@ -94,11 +96,14 @@
     def f_dev(k):
         return to(dom, feat_peer(k))
 
-    def remote(src, dst, sems, at, device):
+    def remote(src, dst, sent, came, device):
         return pltpu.make_async_remote_copy(
-            src_ref=src, dst_ref=dst, send_sem=sems.at[0, at], recv_sem=sems.at[1, at],
+            src_ref=src, dst_ref=dst, send_sem=sent, recv_sem=came,
             device_id=device, device_id_type=MESH,
         )
+
+    def wait_for(ref, sem):
+        pltpu.make_async_copy(ref, ref, sem).wait()
 
     def loop(lower, upper, body):
         def step(i, carry):
@@ -119,7 +124,7 @@
     greet(to(prv, me))
     loop(1, nf, lambda k: greet(f_dev(k)))
     x_loads = [
-        pltpu.make_async_copy(x.at[:, pl.ds(128 * b, 128)], ext.at[nb + b], s_x.at[b])
+        pltpu.make_async_copy(x.at[:, pl.ds(128 * b, 128)], ext.at[nb + b], s_x)
         for b in range(nb)
     ]
     for copy in x_loads:
@@ -127,7 +132,7 @@
     tiles_load = pltpu.make_async_copy(tiles, tiles_f32, s_misc.at[0])
     w_load = pltpu.make_async_copy(w, w_f32, s_misc.at[1])
     adj_loads = [
-        pltpu.make_async_copy(hub_adj.at[:, pl.ds(vw * p, vw)], adj_f32.at[p], s_adj.at[p])
+        pltpu.make_async_copy(hub_adj.at[:, pl.ds(vw * p, vw)], adj_f32.at[p], s_adj)
         for p in range(nf)
     ]
     cot_own = pltpu.make_async_copy(
@@ -140,27 +145,28 @@
     for copy in adj_loads:
         copy.start()
 
-    for copy in x_loads:
-        copy.wait()
-
-    half = nb // 2
+    wait_for(ext.at[pl.ds(nb, nb)], s_x)
+
+    quarter = nb // 4
 
     def ext_copy(side, h):
         at, device = ((0, to(nxt, me)), (2 * nb, to(prv, me)))[side]
         return remote(
-            ext.at[pl.ds(nb + half * h, half)], ext.at[pl.ds(at + half * h, half)],
-            s_nbr.at[h], side, device,
-        )
-
-    def both_sides(copies, h):
-        copies(0, h).start()
-        copies(1, h).start()
+            ext.at[pl.ds(nb + quarter * h, quarter)], ext.at[pl.ds(at + quarter * h, quarter)],
+            s_nbr.at[0], s_nbr.at[1], device,
+        )
+
+    def both_sides(copies, which):
+        for h in which:
+            copies(0, h).start()
+            copies(1, h).start()
 
     def cot_copy(k):
         p = feat_peer(k)
         return remote(
             cot.at[:, pl.ds(pl.multiple_of(vw * p, 128), vw)],
-            cot_all.at[pl.ds(pl.multiple_of(fl * me, 8), fl), :], s_cot, k - 1, f_dev(k),
+            cot_all.at[pl.ds(pl.multiple_of(fl * me, 8), fl), :], s_cot.at[0], s_cot.at[1],
+            f_dev(k),
         )
 
     local_id = ids[...] - dom * vl
@@ -199,19 +205,21 @@
     def x_rs_copy(s, k, h):
         at = piece(h)
         return remote(
-            h_src.at[s, x_peer(k), at], h_rx.at[s, k - 1, at], s_hx.at[s, h], k - 1, x_dev(k)
+            h_src.at[s, x_peer(k), at], h_rx.at[s, k - 1, at], s_hx.at[s, 3], s_hx.at[s, h],
+            x_dev(k),
         )
 
     def z_rs_copy(s, o):
-        return remote(h_zsrc.at[s, o], h_rz.at[s, o], s_hz.at[s], o, z_dev(z_step(o)))
-
-    def z_ag_copy(s, o):
+        sent, came = s_hz.at[s, 0], s_hz.at[s, 1]
+        return remote(h_zsrc.at[s, o], h_rz.at[s, o], sent, came, z_dev(z_step(o)))
+
+    def z_ag_copy(s, o, h):
         dst = h_zg.at[s, z_back(o)]
-        return remote(h_zg.at[s, own_at], dst, s_hzg.at[s], o, z_dev(z_step(o)))
+        return remote(h_zg.at[s, own_at], dst, s_hzg.at[s, 3], s_hzg.at[s, h], z_dev(z_step(o)))
 
     def x_ag_copy(s, k, h):
         at = piece(h)
-        return remote(h_zg.at[s, at], h_xg.at[s, k, at], s_hxg.at[s, h], k - 1, x_dev(k))
+        return remote(h_zg.at[s, at], h_xg.at[s, k, at], s_hxg.at[s, 0], s_hxg.at[s, 1], x_dev(k))
 
     x_order = [2, 1, 3][:nx] if nx > 2 else [1]
 
@@ -232,9 +240,8 @@
 
     def hub_z(s):
         for h in range(len(pieces)):
-            for k in x_order:
-                x_rs_copy(s, k, h).wait_recv()
             at = piece(h)
+            wait_for(h_rx.at[s, :, at], s_hx.at[s, h])
             total = h_src[s, my_x, at]
             for k in range(1, nx):
                 total += h_rx[s, k - 1, at]
@@ -242,24 +249,25 @@
             z_loop(h, lambda o: z_rs_copy(s, o).start())
 
     def hub_zg(s):
-        loop(0, nz - 1, lambda o: z_rs_copy(s, o).wait_recv())
+        wait_for(h_rz.at[s], s_hz.at[s, 1])
         total = h_zsrc[s, own_at]
         for o in range(nz - 1):
             total += h_rz[s, o]
         h_zg[s, own_at] = total
-        loop(0, nz - 1, lambda o: z_ag_copy(s, o).start())
+        for h in range(len(pieces)):
+            z_loop(h, lambda o: z_ag_copy(s, o, h).start())
 
     def hub_xg(s, h):
-        z_loop(h, lambda o: z_ag_copy(s, o).wait_recv())
+        lower, upper = pieces[h]
+        if min(upper, nz - 1) > lower:
+            wait_for(h_zg.at[s, pl.ds(lower, min(upper, nz - 1) - lower)], s_hzg.at[s, h])
         for k in x_order:
             x_ag_copy(s, k, h).start()
         at = piece(h)
         h_xg[s, 0, at] = h_zg[s, at]
 
     def hub_end(s):
-        for h in reversed(range(len(pieces))):
-            for k in x_order:
-                x_ag_copy(s, k, h).wait_recv()
+        wait_for(h_xg.at[s, pl.ds(1, nx - 1)], s_hxg.at[s, 1])
         for q in range(nx):
             for i in range(nz):
                 r, c = i // per_q, q * per_q + i % per_q
@@ -268,6 +276,7 @@
         hub_in[...] = stacked(hub_acc[...])
 
     hub_start(0)
+    both_sides(ext_copy, THERE[0])
     tiles_load.wait()
 
     def split_tiles(b):
@@ -277,7 +286,7 @@
 
     loop(0, nb, split_tiles)
     hub_z(0)
-    both_sides(ext_copy, 0)
+    both_sides(ext_copy, THERE[1])
     loop(1, nf, lambda k: cot_copy(k).start())
 
     entries = nb * slots
@@ -328,19 +337,16 @@
         adj_hi[p] = high
         adj_lo[p] = low
 
-    for copy in adj_loads:
-        copy.wait()
+    wait_for(adj_f32, s_adj)
     loop(0, nf // 2, split_adj)
     hub_zg(0)
-    both_sides(ext_copy, 1)
+    both_sides(ext_copy, THERE[2])
     loop(nf // 2, nf, split_adj)
     order_copy.wait()
     for h in reversed(range(len(pieces))):
         hub_xg(0, h)
 
-    for h in range(2):
-        ext_copy(0, h).wait_recv()
-        ext_copy(1, h).wait_recv()
+    wait_for(ext.at[pl.ds(0, 2 * nb)], s_nbr.at[1])
 
     def tile_part(p):
         for j in range(pb):
@@ -349,85 +355,86 @@
                 [ext[cols[k, b]] * jnp.where(k < count[b], 1.0, 0.0) for k in range(slots)],
                 axis=1,
             )
-            y_send[p, :, 128 * j : 128 * j + 128] = mm3(stacked(left), cat_hi[b], cat_lo[b], NT)
+            y_send[j, p] = mm3(stacked(left), cat_hi[b], cat_lo[b], NT)
 
     loop(0, nf, tile_part)
     hub_end(0)
 
-    def y_copy(k):
+    def rows_of(p):
+        return pl.ds(pl.multiple_of(fl * p, 8), fl)
+
+    def y_copy(j, k):
         return remote(
-            y_send.at[feat_peer(k)], y_all.at[pl.ds(pl.multiple_of(fl * me, 8), fl), :],
-            s_y, k - 1, f_dev(k),
-        )
-
-    def y_recv(k):
-        at = y_all.at[pl.ds(pl.multiple_of(fl * feat_from(k), 8), fl), :]
-        return remote(y_send.at[0], at, s_y, k - 1, f_dev(k))
-
-    def hub_to_y(p):
-        return y_send[p] + mm3(hub_in[...], adj_hi[p], adj_lo[p], NN)
+            y_send.at[j, feat_peer(k)], y_all.at[j, rows_of(me)], s_y.at[j, 0], s_y.at[j, 1],
+            f_dev(k),
+        )
 
     def feat_order(i):
         return nf // 2 if nf < 4 else (nf // 2 + (1 - 2 * (i % 2)) * ((i + 1) // 2)) % nf
+
+    def to_feats(copies, j):
+        loop(0, nf - 1, lambda i: copies(j, feat_order(i)).start())
 
     def hub_part(i):
         k = feat_order(i)
         p = feat_peer(k)
-        y_send[p] = hub_to_y(p)
-        y_copy(k).start()
+        part = mm3(hub_in[...], adj_hi[p], adj_lo[p], NN)
+        for j in range(pb):
+            y_send[j, p] += part[:, 128 * j : 128 * j + 128]
+        y_copy(0, k).start()
 
     loop(0, nf - 1, hub_part)
-    y_all[pl.ds(pl.multiple_of(fl * me, 8), fl), :] = hub_to_y(me)
-
-    loop(1, nf, lambda k: y_recv(k).wait_recv())
-    y_hi, y_lo = split(y_all[...])
-    agg = mm3(wt_st[...], y_hi, y_lo, NN)
-    sig = 1.0 / (1.0 + jnp.exp(-agg))
-    act_send[...] = agg * sig
+    for j in range(1, pb):
+        to_feats(y_copy, j)
+    part = mm3(hub_in[...], adj_hi[me], adj_lo[me], NN)
+    for j in range(pb):
+        y_all[j, rows_of(me)] = y_send[j, me] + part[:, 128 * j : 128 * j + 128]
+
     cot_own.wait()
 
-    def cot_recv(k):
-        at = cot_all.at[pl.ds(pl.multiple_of(fl * feat_from(k), 8), fl), :]
-        return remote(cot.at[:, pl.ds(0, vw)], at, s_cot, k - 1, f_dev(k))
-
-    loop(1, nf, lambda k: cot_recv(k).wait_recv())
-    grad = cot_all[...] * sig * (1.0 + agg * (1.0 - sig))
-    g_hi, g_lo = split(grad)
-    q_send[...] = mm3(w_st[...], g_hi, g_lo, NN)
-
-    def rows_of(ref, p):
-        return ref.at[pl.ds(pl.multiple_of(fl * p, 8), fl), :]
-
-    def q_copy(k):
-        return remote(rows_of(q_send, feat_peer(k)), q_all.at[me], s_q, k - 1, f_dev(k))
-
-    def q_recv(k):
-        return remote(rows_of(q_send, me), q_all.at[feat_from(k)], s_q, k - 1, f_dev(k))
-
-    loop(0, nf - 1, lambda i: q_copy(feat_order(i)).start())
-    q_all[me] = q_send[pl.ds(pl.multiple_of(fl * me, 8), fl), :]
-
-    g_st = jnp.concatenate([g_hi, g_lo], axis=0)
+    others = pl.ds(0, fl * (nf - 1))
+    wait_for(cot_all.at[others, :], s_cot.at[1])
+
+    def q_copy(j, k):
+        at = q_all.at[me, :, pl.ds(128 * j, 128)]
+        src = q_send.at[j, rows_of(feat_peer(k))]
+        return remote(src, at, s_q.at[0], s_q.at[k], f_dev(k))
+
+    y_parts, g_parts = [], []
+    for j in range(pb):
+        cols_j = slice(128 * j, 128 * j + 128)
+        wait_for(y_all.at[j, others], s_y.at[j, 1])
+        y_hi, y_lo = split(y_all[j])
+        agg = mm3(wt_st[...], y_hi, y_lo, NN)
+        sig = 1.0 / (1.0 + jnp.exp(-agg))
+        act_send[:, cols_j] = agg * sig
+        grad = cot_all[:, cols_j] * sig * (1.0 + agg * (1.0 - sig))
+        g_hi, g_lo = split(grad)
+        q_send[j] = mm3(w_st[...], g_hi, g_lo, NN)
+        to_feats(q_copy, j)
+        q_all[me, :, cols_j] = q_send[j, rows_of(me)]
+        y_parts.append((y_hi, y_lo))
+        g_parts.append(jnp.concatenate([g_hi, g_lo], axis=0))
+
+    g_st = jnp.concatenate(g_parts, axis=1)
+    y_hi, y_lo = [jnp.concatenate(one_part, axis=1) for one_part in zip(*y_parts)]
     terms = mm3(g_st, y_hi, y_lo, NT)
     for p in range(nf):
         wg_src[p % 2, p // 2] = terms[fl * p : fl * p + fl]
-    pair = remote(wg_src.at[1 - my_core], wg_pair, s_wp, 0, to(dom, me + 1 - 2 * my_core))
+    pair = remote(wg_src.at[1 - my_core], wg_pair, s_wp.at[0], s_wp.at[1], to(dom, me + 1 - 2 * my_core))
     pair.start()
 
     def wf_copy(k):
         y = (my_y + k) % ny
-        return remote(wg_half.at[y], wg_recv.at[k - 1], s_wf, k - 1, to(dom, y * 2 + my_core))
+        return remote(wg_half.at[y], wg_recv.at[k - 1], s_wf.at[0], s_wf.at[1], to(dom, y * 2 + my_core))
 
     def act_at(p):
         return act.at[:, pl.ds(pl.multiple_of(vw * p, 128), vw)]
 
     def act_copy(k):
-        return remote(rows_of(act_send, feat_peer(k)), act_at(me), s_act, k - 1, f_dev(k))
-
-    def act_recv(k):
-        return remote(rows_of(act_send, me), act_at(feat_from(k)), s_act, k - 1, f_dev(k))
-
-    act_own = pltpu.make_async_copy(rows_of(act_send, me), act_at(me), s_misc.at[3])
+        return remote(act_send.at[rows_of(feat_peer(k)), :], act_at(me), s_act.at[0], s_act.at[1], f_dev(k))
+
+    act_own = pltpu.make_async_copy(act_send.at[rows_of(me), :], act_at(me), s_misc.at[3])
     act_own.start()
 
     def hub_back(p):
@@ -437,7 +444,7 @@
     hub_acc[...] = hub_back(me)
 
     def hub_step(k):
-        q_recv(k).wait_recv()
+        wait_for(q_all.at[feat_from(k)], s_q.at[k])
         hub_acc[...] += hub_back(feat_from(k))
 
     loop(1, nf, hub_step)
@@ -474,33 +481,34 @@
     loop(0, nb, back_send)
 
     def back_copy(side, h):
-        at = pl.ds(half * h, half)
+        at = pl.ds(quarter * h, quarter)
         device = (to(prv, me), to(nxt, me))[side]
-        return remote(b_send.at[side, at], b_recv.at[side, at], s_back.at[h], side, device)
-
+        return remote(b_send.at[side, at], b_recv.at[side, at], s_back.at[0], s_back.at[1], device)
+
+    both_sides(back_copy, BACK[0])
     hub_z(1)
-    both_sides(back_copy, 0)
+    both_sides(back_copy, BACK[1])
 
     term = wg_half[my_y]
+    if ny > 1:
+        wait_for(wg_recv, s_wf.at[1])
     for k in range(1, ny):
-        wf_copy(k).wait_recv()
         term += wg_recv[k - 1]
     part = full // nx
     for q in range(nx):
         wg_xsrc[q] = term[:, part * q : part * q + part]
 
     def wx_copy(k):
-        return remote(wg_xsrc.at[x_peer(k)], wg_rx.at[k - 1], s_wx, k - 1, x_dev(k))
+        return remote(wg_xsrc.at[x_peer(k)], wg_rx.at[k - 1], s_wx.at[0], s_wx.at[1], x_dev(k))
 
     for k in range(1, nx):
         wx_copy(k).start()
 
     hub_zg(1)
-    both_sides(back_copy, 1)
+    both_sides(back_copy, BACK[2])
     loop(0, nf - 1, lambda i: act_copy(feat_order(i)).start())
 
-    for k in range(1, nx):
-        wx_copy(k).wait_recv()
+    wait_for(wg_rx, s_wx.at[1])
     term = wg_xsrc[my_x]
     for k in range(1, nx):
         term += wg_rx[k - 1]
@@ -511,7 +519,7 @@
     wg_zsrc[...] = term.reshape(wg_zsrc.shape)
 
     def wz_copy(k):
-        return remote(wg_zsrc.at[z_peer(k)], wg_rz.at[k - 1], s_wz, k - 1, z_dev(k))
+        return remote(wg_zsrc.at[z_peer(k)], wg_rz.at[k - 1], s_wz.at[0], s_wz.at[1], z_dev(k))
 
     loop(1, nz, lambda k: wz_copy(k).start())
 
@@ -520,13 +528,11 @@
 
 
     hub_end(1)
-    for h in range(2):
-        back_copy(0, h).wait_recv()
-        back_copy(1, h).wait_recv()
+    wait_for(b_recv, s_back.at[1])
 
     def out_copy(p):
         return pltpu.make_async_copy(
-            fg_out.at[p], fg.at[:, pl.ds(pl.multiple_of(vw * p, 128), vw)], s_out.at[p]
+            fg_out.at[p], fg.at[:, pl.ds(pl.multiple_of(vw * p, 128), vw)], s_out
         )
 
     def finish(p):
@@ -541,44 +547,32 @@
 
     loop(0, nf, finish)
 
-    loop(1, nz, lambda k: wz_copy(k).wait_recv())
+    wait_for(wg_rz, s_wz.at[1])
     term = wg_zsrc[my_z]
     for k in range(1, nz):
         term += wg_rz[k - 1]
     wg[...] = term[:, :fl] * (1.0 / math.sqrt(vl * nd))
 
     act_own.wait()
-    loop(1, nf, lambda k: act_recv(k).wait_recv())
+    wait_for(act.at[:, pl.ds(0, vw * (nf - 1))], s_act.at[1])
     pair.wait_send()
-    for h in range(2):
-        for side in range(2):
-            ext_copy(side, h).wait_send()
-            back_copy(side, h).wait_send()
-    for k in range(1, ny):
-        wf_copy(k).wait_send()
-
-    def feat_sent(k):
-        cot_copy(k).wait_send()
-        y_copy(k).wait_send()
-        q_copy(k).wait_send()
-        act_copy(k).wait_send()
-
-    loop(1, nf, feat_sent)
-    for k in range(1, nx):
-        for s in range(2):
-            for h in range(len(pieces)):
-                x_rs_copy(s, k, h).wait_send()
-                x_ag_copy(s, k, h).wait_send()
-        wx_copy(k).wait_send()
-
-    def z_sent(o):
-        for s in range(2):
-            z_rs_copy(s, o).wait_send()
-            z_ag_copy(s, o).wait_send()
-        wz_copy(o + 1).wait_send()
-
-    loop(0, nz - 1, z_sent)
-    loop(0, nf, lambda p: out_copy(p).wait())
+    wait_for(ext.at[pl.ds(0, 2 * nb)], s_nbr.at[0])
+    wait_for(b_send, s_back.at[0])
+    wait_for(cot_all.at[others, :], s_cot.at[0])
+    for j in range(pb):
+        wait_for(y_all.at[j, others], s_y.at[j, 0])
+    wait_for(q_all.at[pl.ds(0, nf - 1)], s_q.at[0])
+    wait_for(act_send.at[others, :], s_act.at[0])
+    if ny > 1:
+        wait_for(wg_recv, s_wf.at[0])
+    wait_for(wg_rx, s_wx.at[0])
+    wait_for(wg_rz, s_wz.at[0])
+    for s in range(2):
+        wait_for(h_rx.at[s], s_hx.at[s, 3])
+        wait_for(h_rz.at[s], s_hz.at[s, 0])
+        wait_for(h_rz.at[s], s_hzg.at[s, 3])
+        wait_for(h_xg.at[s, pl.ds(1, nx - 1)], s_hxg.at[s, 0])
+    wait_for(fg_out, s_out)
 
 
 def hand_over_kernel(count, *refs):
@@ -617,7 +611,7 @@
     nh = hub_adj.shape[0]
     vw = vl // nf
     entries = nb * slots
-    ny = nf // 2
+    ny, pb = nf // 2, nb // nf
     lanes = max(fl, 128)
     vm = pltpu.VMEM
     dma = pltpu.SemaphoreType.DMA
@@ -629,8 +623,8 @@
         vm((nb, 128, slots * 128), BF16), vm((nb, 128, slots * 128), BF16),
         vm((nf, vw, nh), BF16),
         vm((full, full), F32), vm((2 * full, full), BF16), vm((2 * full, full), BF16),
-        vm((nf, fl, vw), F32), vm((full, vw), F32), vm((full, vw), F32), vm((full, vw), F32),
-        vm((full, vw), F32), vm((nf, fl, vw), F32),
+        vm((pb, nf, fl, 128), F32), vm((pb, full, 128), F32), vm((full, vw), F32),
+        vm((full, vw), F32), vm((pb, full, 128), F32), vm((nf, fl, vw), F32),
         vm((fl, nh), F32), vm((2 * fl, nh), BF16),
         vm((entries, fl, 128), F32), vm((entries, fl, 128), F32),
         vm((2, nb, fl, 128), F32), vm((2, nb, fl, 128), F32), vm((nf, fl, vw), F32),
@@ -642,11 +636,10 @@
         vm((max(ny - 1, 1), fl, full), F32),
         vm((nx, fl, full // nx), F32), vm((nx - 1, fl, full // nx), F32),
         vm((nz, full // nx // nz, lanes), F32), vm((nz - 1, full // nx // nz, lanes), F32),
-        dma((nb,)), dma((4,)), dma((nf,)), dma, dma((nf,)),
-        dma((2, 2, 2)), dma((2, nf - 1)), dma((2, nf - 1)), dma((2, nf - 1)), dma((2, nf - 1)),
-        dma((2, 2, 2)),
-        dma((2, 3, 2, nx - 1)), dma((2, 2, nz - 1)), dma((2, 2, nz - 1)), dma((2, 3, 2, nx - 1)),
-        dma((2, 1)), dma((2, max(ny - 1, 1))), dma((2, nx - 1)), dma((2, nz - 1)),
+        dma, dma((4,)), dma, dma, dma,
+        dma((2,)), dma((2,)), dma((pb, 2)), dma((nf,)), dma((2,)), dma((2,)),
+        dma((2, 4)), dma((2, 2)), dma((2, 4)), dma((2, 2)),
+        dma((2,)), dma((2,)), dma((2,)), dma((2,)),
     ]
     hbm = pl.BlockSpec(memory_space=pl.ANY)
     vmem = pl.BlockSpec(memory_space=pltpu.VMEM)

time: 97.7 us -> 94.3 us (0.965)
  Pallas kernels: 96.2 us -> 93.5 us
    pallas_call x1, Pallas kernels: 94.1 us -> 91.4 us  [local(): pl.pallas_call(functools.partial(kernel, (nx, nz, nf, nb, slots)), out_sh...]
where the time goes in v4:
time: 94.3 us; the launch traced here: 94.1 us
  Pallas kernels  93.5 us (99%)
    pallas_call x1, Pallas kernels, local(): pl.pallas_call(functools.partial(kernel, (nx, nz, nf, nb, slots)), out_sh...  91.4 us
    pallas_call x1, Pallas kernels, hand_over(): pl.pallas_call(functools.partial(hand_over_kernel, count), out_shape=tupl...  2.06 us

profile of v4, /device:TPU:1, one launch (start us, length us, event | category | flops | bytes accessed | tf_op | source)
XLA Modules:
  0.0 94.1 jit_solution(3702465168009477533)
XLA Ops:
  0.6 91.4 %shard_map.103 = (f32[64,2048]{1,0:T(8,128)}, f32[64,2048]{1,0:T(8,128)}, f32[8,64]{1,0:T(8,128)}) custom-call(f32[64,2048]{1,0:T(8,128)} %x.1, f32[512,512]{1,0:T(8,128)} %w.1, f32[16,4,128,128]{3,2,1,0:T(8,128)} %tiles.1, f32[1024,2048]{1,0:T(8,128)} %hub_adj.1, f32[64,2048]{1,0:T(8,128)} %cot.1, s32[8,128]{1,0:T(8,128)} %bitcast.4, s32[4,16]{1,0:T(4,128)} %bitcast.2, ...), custom_call_target="tpu_custom_call" | custom-call | tf_op jit(solution)/shard_map/pallas_call | solution.py:647
  92.1 2.1 %shard_map.104 = (f32[64,2048]{1,0:T(8,128)}, f32[64,2048]{1,0:T(8,128)}, f32[8,64]{1,0:T(8,128)}) custom-call(f32[64,2048]{1,0:T(8,128)} %get-tuple-element.6.refs_0_, f32[64,2048]{1,0:T(8,128)} %get-tuple-element.7.refs_1_, f32[8,64]{1,0:T(8,128)} %get-tuple-element.8.refs_2_), custom_call_target="tpu_custom_call" | custom-call | tf_op jit(solution)/shard_map/pallas_call | solution.py:595

commit v5 on v4

--- a/solution.py
+++ b/solution.py
@@ -40,14 +40,14 @@
 
 def kernel(
     sizes,
-    x, w, tiles, hub_adj, cot, ids, cols_v, cols, count,
+    x, w, tiles, hub_adj, cot, ids_at, cols_at, count_at,
     act, fg, wg,
-    ext, adj_f32, adj_hi, adj_lo, tiles_f32, cat_hi, cat_lo, pick,
+    ids, cols_v, cols, count, ext, adj_f32, adj_hi, adj_lo, tiles_f32, cat_hi, cat_lo, pick,
     w_f32, w_st, wt_st, y_send, y_all, cot_all, act_send, q_send, q_all,
     hub_acc, hub_in, contrib, runs, b_send, b_recv, fg_out, order_v, order,
     h_src, h_rx, h_zsrc, h_rz, h_zg, h_xg,
     wg_src, wg_pair, wg_half, wg_recv, wg_xsrc, wg_rx, wg_zsrc, wg_rz,
-    s_x, s_misc, s_adj, s_cot_own, s_out,
+    s_small, s_x, s_misc, s_adj, s_cot_own, s_out,
     s_nbr, s_cot, s_y, s_q, s_act, s_back, s_hx, s_hz, s_hzg, s_hxg, s_wp, s_wf, s_wx, s_wz,
 ):
     nx, nz, nf, nb, slots = sizes
@@ -123,6 +123,14 @@
     greet(to(nxt, me))
     greet(to(prv, me))
     loop(1, nf, lambda k: greet(f_dev(k)))
+    small = [
+        pltpu.make_async_copy(ids_at, ids, s_small.at[0]),
+        pltpu.make_async_copy(cols_at, cols_v, s_small.at[1]),
+        pltpu.make_async_copy(cols_at, cols, s_small.at[2]),
+        pltpu.make_async_copy(count_at, count, s_small.at[3]),
+    ]
+    for copy in small:
+        copy.start()
     x_loads = [
         pltpu.make_async_copy(x.at[:, pl.ds(128 * b, 128)], ext.at[nb + b], s_x)
         for b in range(nb)
@@ -145,7 +153,6 @@
     for copy in adj_loads:
         copy.start()
 
-    wait_for(ext.at[pl.ds(nb, nb)], s_x)
 
     quarter = nb // 4
 
@@ -169,21 +176,27 @@
             f_dev(k),
         )
 
+    for copy in small:
+        copy.wait()
     local_id = ids[...] - dom * vl
     hub_acc[...] = jnp.zeros_like(hub_acc)
 
-    def own_hubs(p):
+    def select(p):
         row = lax.broadcasted_iota(jnp.int32, (vw, 128), 0) + p * vw
-        chunk = jnp.concatenate(
+        pick[p] = jnp.concatenate(
             [
                 jnp.where(row == local_id[g : g + 1], 1.0, 0.0).astype(BF16)
                 for g in range(nh // 128)
             ],
             axis=1,
         )
-        pick[p] = chunk
+
+    loop(0, nf, select)
+    wait_for(ext.at[pl.ds(nb, nb)], s_x)
+
+    def own_hubs(p):
         left = stacked(jnp.concatenate([ext[nb + pb * p + j] for j in range(pb)], axis=1))
-        both = mm(left, chunk, NN)
+        both = mm(left, pick[p], NN)
         hub_acc[...] += both[:fl] + both[fl:]
 
     loop(0, nf, own_hubs)
@@ -527,8 +540,15 @@
         hub_xg(1, h)
 
 
+    wait_for(b_recv, s_back.at[1])
+
+    def near_sum(p):
+        for j in range(pb):
+            b = p * pb + j
+            fg_out[p, :, 128 * j : 128 * j + 128] = summed(nb + b) + b_recv[0, b] + b_recv[1, b]
+
+    loop(0, nf, near_sum)
     hub_end(1)
-    wait_for(b_recv, s_back.at[1])
 
     def out_copy(p):
         return pltpu.make_async_copy(
@@ -537,12 +557,7 @@
 
     def finish(p):
         both = mm(hub_in[...], pick[p], NT)
-        placed = both[:fl] + both[fl:]
-        for j in range(pb):
-            b = p * pb + j
-            own = summed(nb + b)
-            total = placed[:, 128 * j : 128 * j + 128] + own + b_recv[0, b] + b_recv[1, b]
-            fg_out[p, :, 128 * j : 128 * j + 128] = total
+        fg_out[p] += both[:fl] + both[fl:]
         out_copy(p).start()
 
     loop(0, nf, finish)
@@ -617,6 +632,8 @@
     dma = pltpu.SemaphoreType.DMA
     hub_tile = (8, 128)
     scratch = [
+        vm((nh // 128, 128), jnp.int32), vm((slots, nb), jnp.int32),
+        pltpu.SMEM((slots, nb), jnp.int32), pltpu.SMEM((nb,), jnp.int32),
         vm((3 * nb, fl, 128), F32),
         vm((nf, nh, vw), F32), vm((nf, nh, vw), BF16), vm((nf, nh, vw), BF16),
         vm((nb, slots, 128, 128), F32),
@@ -636,14 +653,13 @@
         vm((max(ny - 1, 1), fl, full), F32),
         vm((nx, fl, full // nx), F32), vm((nx - 1, fl, full // nx), F32),
         vm((nz, full // nx // nz, lanes), F32), vm((nz - 1, full // nx // nz, lanes), F32),
-        dma, dma((4,)), dma, dma, dma,
+        dma((4,)), dma, dma((4,)), dma, dma, dma,
         dma((2,)), dma((2,)), dma((pb, 2)), dma((nf,)), dma((2,)), dma((2,)),
         dma((2, 4)), dma((2, 2)), dma((2, 4)), dma((2, 2)),
         dma((2,)), dma((2,)), dma((2,)), dma((2,)),
     ]
     hbm = pl.BlockSpec(memory_space=pl.ANY)
     vmem = pl.BlockSpec(memory_space=pltpu.VMEM)
-    smem = pl.BlockSpec(memory_space=pltpu.SMEM)
     results = pl.pallas_call(
         functools.partial(kernel, (nx, nz, nf, nb, slots)),
         out_shape=(
@@ -651,7 +667,7 @@
             jax.ShapeDtypeStruct((fl, vl), F32),
             jax.ShapeDtypeStruct((full // nd, fl), F32),
         ),
-        in_specs=[hbm] * 5 + [vmem] * 2 + [smem] * 2,
+        in_specs=[hbm] * 8,
         out_specs=(hbm, hbm, vmem),
         scratch_shapes=scratch,
         compiler_params=pltpu.CompilerParams(
@@ -659,7 +675,7 @@
         ),
     )(
         node_feats, weight, tiles, hub_adj, cotangent, hub_ids.reshape(nh // 128, 128),
-        block_cols.T, block_cols.T, block_count,
+        block_cols.T, block_count,
     )
     return hand_over(results)
 

time: 94.3 us -> 92.1 us (0.977)
  Pallas kernels: 93.5 us -> 91.2 us
    pallas_call x1, Pallas kernels: 91.4 us -> 89.2 us  [local(): pl.pallas_call(functools.partial(kernel, (nx, nz, nf, nb, slots)), out_sh...]
where the time goes in v5:
time: 92.1 us; the launch traced here: 91.9 us
  Pallas kernels  91.2 us (99%)
    pallas_call x1, Pallas kernels, local(): pl.pallas_call(functools.partial(kernel, (nx, nz, nf, nb, slots)), out_sh...  89.2 us
    pallas_call x1, Pallas kernels, hand_over(): pl.pallas_call(functools.partial(hand_over_kernel, count), out_shape=tupl...  2.06 us

profile of v5, /device:TPU:1, one launch (start us, length us, event | category | flops | bytes accessed | tf_op | source)
XLA Modules:
  0.0 91.9 jit_solution(17109634383151920753)
XLA Ops:
  0.6 89.2 %shard_map.103 = (f32[64,2048]{1,0:T(8,128)}, f32[64,2048]{1,0:T(8,128)}, f32[8,64]{1,0:T(8,128)}) custom-call(f32[64,2048]{1,0:T(8,128)} %x.1, f32[512,512]{1,0:T(8,128)} %w.1, f32[16,4,128,128]{3,2,1,0:T(8,128)} %tiles.1, f32[1024,2048]{1,0:T(8,128)} %hub_adj.1, f32[64,2048]{1,0:T(8,128)} %cot.1, s32[8,128]{1,0:T(8,128)} %bitcast.2, s32[4,16]{1,0:T(4,128)} %bitcast.3, ...), custom_call_target="tpu_custom_call" | custom-call | tf_op jit(solution)/shard_map/pallas_call | solution.py:663
  89.8 2.1 %shard_map.104 = (f32[64,2048]{1,0:T(8,128)}, f32[64,2048]{1,0:T(8,128)}, f32[8,64]{1,0:T(8,128)}) custom-call(f32[64,2048]{1,0:T(8,128)} %get-tuple-element.6.refs_0_, f32[64,2048]{1,0:T(8,128)} %get-tuple-element.7.refs_1_, f32[8,64]{1,0:T(8,128)} %get-tuple-element.8.refs_2_), custom_call_target="tpu_custom_call" | custom-call | tf_op jit(solution)/shard_map/pallas_call | solution.py:610
